TPU v7x, 128 devices: a whole 4x4x4 slice. The times are simulated.
128 devices in a mesh: cfg: 2 (over core), blk: 8 (over x_lo, y), sp: 8 (over z, x_hi).
Axes of the slice: x: 4 (x_hi: 2, x_lo: 2; x = x_hi * 2 + x_lo), y: 4, z: 4, core: 2. Of those that a mesh axis runs over, the one named last changes fastest.
Arguments:
- qkv: bfloat16 [2, 16, 512, 9216], P('cfg', 'blk', 'sp'), may hold values from -130 to 130
- residual: bfloat16 [2, 16, 512, 3072], P('cfg', 'blk', 'sp'), may hold values from -4 to 4
- text_kv: bfloat16 [2, 256, 2, 24, 128], P('cfg'), may hold values from -16 to 16
- text_len: int32 [2], P('cfg'), may hold values from 128 to 256
- text_keep: int32 [2, 256], P('cfg'), may hold values 0 or 1
- attn_gate: float32 [2, 3072], P('cfg'), may hold values from 1 to 3
- w_out: bfloat16 [3072, 3072], replicated, may hold values from -0.109375 to 0.109375
- final_mod: float32 [2, 2, 3072], P('cfg'), may hold values from -3 to 3
- w_final: bfloat16 [3072, 64], replicated, may hold values from -0.109375 to 0.109375
- noisy: float32 [16, 512, 64], P('blk', 'sp'), may hold values from -6 to 6
- conv_weight: bfloat16 [3, 16, 512], replicated, may hold values from -0.875 to 0.875
- conv_bias: float32 [512], replicated, may hold values from -3 to 3
Outputs:
- velocity: float32 [16, 512, 64], P('blk', 'sp')
- decoded: bfloat16 [16, 512, 4, 512], P('blk', 'sp', 'cfg')
All inputs are finite; a program needn't handle non-finite values. No bound on the sum of `text_keep` on one device may be relied on, other than what follows from the above.
Results may differ from a plain program's by a relative error of at most 0.012.
Values may be sent and summed in bfloat16 or wider, within the bound.
A program may use at most 128 MiB of HBM per device.

v0:
```python
import math

import jax
import jax.numpy as jnp
from jax import lax
from jax.sharding import PartitionSpec as P

D = 3072
H = 24
HD = 128


guidance_scale = 6.0
sigma_last = 0.125
vae_factor = 0.476986
norm_eps = 1e-06


def swapped(block, axis, distance):
    count = lax.axis_size(axis)
    route = []
    for low in range(count):
        high = low | 1 << distance
        if high != low and high < count:
            route += [(low, high), (high, low)]
    return lax.ppermute(block, axis, route)


def shifted(value, axis, steps):
    count = lax.axis_size(axis)
    leading, last = (max(0, -steps), min(count, count - steps))
    return lax.ppermute(value, axis, [(source, source + steps) for source in range(leading, last)])


def fold_block(running, block_keys, block_values, queries, key_mask):
    old_max, old_sum, old_acc = running
    scores = jnp.einsum(
        "qhd,khd->hqk", queries, block_keys, preferred_element_type=jnp.float32
    ) / math.sqrt(HD)
    if key_mask is not None:
        scores = jnp.where(key_mask, scores, -1e30)
    new_max = jnp.maximum(old_max, jnp.max(scores, axis=-1))
    weights = jnp.exp(scores - new_max[..., None])
    if key_mask is not None:
        weights = jnp.where(key_mask, weights, 0.0)
    factor = jnp.exp(old_max - new_max)
    new_sum = old_sum * factor + jnp.sum(weights, axis=-1)
    new_acc = old_acc * jnp.transpose(factor)[..., None] + jnp.einsum(
        "hqk,khd->qhd",
        weights.astype(jnp.bfloat16),
        block_values,
        preferred_element_type=jnp.float32,
    )
    return (new_max, new_sum, new_acc)


def attention_setup(heads_view, text_kv, text_mask, head_offset, local_heads):
    queries = heads_view[0, :, :, 0].reshape(-1, local_heads, HD)
    row_count = queries.shape[0]
    text_slab = lax.dynamic_slice_in_dim(text_kv[0], head_offset, local_heads, axis=2)
    initial = (
        jnp.full((local_heads, row_count), -1e30, jnp.float32),
        jnp.zeros((local_heads, row_count), jnp.float32),
        jnp.zeros((row_count, local_heads, HD), jnp.float32),
    )
    started = fold_block(initial, text_slab[:, 0], text_slab[:, 1], queries, text_mask)

    def visit(running, shard_kv, first_row):
        blocks = shard_kv.reshape(-1, row_count, 2, local_heads, HD)

        def step_block(state_now, block_kv):
            return (fold_block(state_now, block_kv[:, 0], block_kv[:, 1], queries, None), None)

        result, unused = lax.scan(step_block, running, blocks)
        return result

    return (started, visit)


def finish_heads(final, heads_view, local_heads):
    attended = (final[2] / jnp.transpose(final[1])[..., None]).astype(jnp.bfloat16)
    return attended.reshape(1, heads_view.shape[1], heads_view.shape[2], local_heads, HD)


def to_latent(velocity, noisy):
    return ((noisy - sigma_last * velocity) / vae_factor).astype(jnp.bfloat16)


def causal_conv(earlier, latent, conv_weight, conv_bias, sub_start, sub_count):
    joined = jnp.concatenate([earlier, latent], axis=0)
    frames = latent.shape[0]
    pixel_grid = joined.reshape(joined.shape[0], joined.shape[1], -1, 4)
    pixel_grid = lax.dynamic_slice_in_dim(pixel_grid, sub_start, sub_count, axis=3)
    summed = (
        jnp.zeros((frames, latent.shape[1], sub_count, conv_weight.shape[2]), jnp.float32)
        + conv_bias
    )
    for offset in range(3):
        summed = summed + jnp.einsum(
            "fpcx,co->fpxo",
            pixel_grid[offset : offset + frames],
            conv_weight[offset],
            preferred_element_type=jnp.float32,
        )
    return summed


def shards(
    qkv,
    residual,
    text_kv,
    text_len,
    text_keep,
    attn_gate,
    w_out,
    final_mod,
    w_final,
    noisy,
    conv_weight,
    conv_bias,
):
    frames = qkv.shape[1]
    pixels = qkv.shape[2]
    qkv_grid = qkv.reshape(1, frames, pixels, 3, H, HD)
    text_mask = (jnp.arange(text_kv.shape[1], dtype=jnp.int32) < text_len[0]) & (text_keep[0] == 1)
    local_heads = H // lax.axis_size("sp")
    heads_view = lax.all_to_all(qkv_grid, "sp", split_axis=4, concat_axis=2, tiled=True)
    started, visit = attention_setup(
        heads_view, text_kv, text_mask, lax.axis_index("sp") * local_heads, local_heads
    )
    final = visit(
        started, lax.all_gather(heads_view[0, :, :, 1:3], "blk", axis=0, tiled=True), jnp.int32(0)
    )
    attended = finish_heads(final, heads_view, local_heads)
    tokens_view = lax.all_to_all(attended, "sp", split_axis=2, concat_axis=3, tiled=True)
    attended_rows = tokens_view.reshape(frames * pixels, D)
    projected = jnp.dot(attended_rows, w_out, preferred_element_type=jnp.float32)
    hidden = residual.reshape(frames * pixels, D).astype(jnp.float32) + attn_gate[0] * projected
    centered = hidden - jnp.mean(hidden, axis=-1, keepdims=True)
    normed = centered * lax.rsqrt(jnp.mean(centered * centered, axis=-1, keepdims=True) + norm_eps)
    modulated = (normed * (1.0 + final_mod[0, 1]) + final_mod[0, 0]).astype(jnp.bfloat16)
    own_prediction = jnp.dot(modulated, w_final, preferred_element_type=jnp.float32).reshape(
        frames, pixels, -1
    )
    is_cond = lax.axis_index("cfg") == 0
    partner_pred = swapped(own_prediction.astype(jnp.bfloat16), "cfg", 0).astype(
        own_prediction.dtype
    )
    cond_pred = jnp.where(is_cond, own_prediction, partner_pred)
    uncond_pred = jnp.where(is_cond, partner_pred, own_prediction)
    velocity = uncond_pred + guidance_scale * (cond_pred - uncond_pred)
    latent = to_latent(velocity, noisy)
    earlier = shifted(latent, "blk", 1)
    decoded = causal_conv(
        earlier, latent, conv_weight, conv_bias, lax.axis_index("cfg") * 2, 2
    ).astype(jnp.bfloat16)
    return (velocity, decoded)


def solution(mesh):
    return jax.shard_map(
        shards,
        mesh=mesh,
        in_specs=(
            P("cfg", "blk", "sp", None),
            P("cfg", "blk", "sp", None),
            P("cfg", None, None, None, None),
            P("cfg"),
            P("cfg", None),
            P("cfg", None),
            P(),
            P("cfg", None, None),
            P(),
            P("blk", "sp", None),
            P(),
            P(),
        ),
        out_specs=(P("blk", "sp", None), P("blk", "sp", "cfg", None)),
        check_vma=False,
    )
```

profile of v0, /device:TPU:3, one launch (start us, length us, event | category | flops | bytes accessed | tf_op | source)
XLA Modules:
  0.0 311.0 jit_solution(17561260277286720329)
XLA Ops:
  7.2 2.3 copy.116
  10.1 37.0 %all_to_all.33 = bf16[1,2,64,3,24,128]{5,2,3,1,0,4:T(8,128)(2,1)S(1)} all-to-all(bf16[1,2,64,3,24,128]{5,2,3,1,0,4:T(8,128)(2,1)S(1)} %copy.84), channel_id=1, replica_groups=mesh['cfg'=2,'blk'=8,'sp'=8] {'sp'}, dimensions={4} | all-to-all | bytes 4718592 | tf_op jit(solution)/shard_map/all_to_all | solution.py:127
  56.2 124.8 %all-gather.3.cloned.1.call-done = bf16[1,16,512,2,3,128]{5,2,4,3,0,1:T(8,128)(2,1)} async-done(((bf16[1,2,512,2,3,128]{5,2,4,3,0,1:T(8,128)(2,1)}), bf16[1,16,512,2,3,128]{5,2,4,3,0,1:T(8,128)(2,1)}) %all-gather.3.cloned.1.call-update) | async-done | bytes 12582928 | tf_op jit(solution)/shard_map/all_gather | solution.py:132
  181.0 10.6 %copy.91 = bf16[1,16,512,2,3,128]{5,2,1,4,3,0:T(8,128)(2,1)} copy(bf16[1,16,512,2,3,128]{5,2,4,3,0,1:T(8,128)(2,1)} %all-gather.3.cloned.1.call-done) | data formatting | bytes 25165824 | tf_op jit(solution)/shard_map/all_gather | solution.py:132
  191.6 65.9 %while.14 = (s32[]{:T(128)}, f32[3,1024]{1,0:T(4,128)S(1)}, f32[3,1024]{1,0:T(4,128)S(1)}, f32[1024,3,128]{0,2,1:T(8,128)S(1)}, bf16[8,1024,2,3,128]{4,1,0,3,2:T...) while((s32[]{:T(128)}, f32[3,1024]{1,0:T(4,128)S(1)}, f32[3,1024]{1,0:T(4,128)S(1)}, ...), condition=%wide.region_5.6_spmd, body=%wide.region_2.5_spmd.sunk | while | flops 1636574208 | bytes 46604368 | solution.py:74
  193.1 1.8 bitcast_reduce_fusion.3
  194.9 2.7 bitcast_add_fusion.3
  197.7 2.1 fusion.61
  201.3 1.8 bitcast_reduce_fusion.3
  203.2 2.7 bitcast_add_fusion.3
  205.9 2.1 fusion.61
  209.6 1.8 bitcast_reduce_fusion.3
  211.4 2.7 bitcast_add_fusion.3
  214.1 2.1 fusion.61
  219.6 2.7 bitcast_add_fusion.3
  222.4 2.1 fusion.61
  227.9 2.7 bitcast_add_fusion.3
  230.6 2.1 fusion.61
  236.1 2.7 bitcast_add_fusion.3
  238.9 2.1 fusion.61
  242.5 1.8 bitcast_reduce_fusion.3
  244.3 2.7 bitcast_add_fusion.3
  247.1 2.1 fusion.61
  252.6 2.7 bitcast_add_fusion.3
  255.3 2.1 fusion.61
  259.1 1.9 divide_convert_fusion
  262.7 6.0 %all-to-all-start.1 = ((bf16[1,2,512,3,128]{4,1,3,0,2:T(2,128)(2,1)}), bf16[1,2,512,3,128]{4,1,3,0,2:T(2,128)(2,1)S(1)}, u32[]{:S(2)}, u32[]{:S(2)}) async-start(bf16[1,2,512,3,128]{4,1,3,0,2:T(2,128)(2,1)} %copy.94), calls=%async_computation.1 | async-start | bytes 1572864 | tf_op jit(solution)/shard_map/all_to_all | solution.py:135
  268.8 13.1 %all-to-all-done.1 = bf16[1,2,512,3,128]{4,1,3,0,2:T(2,128)(2,1)S(1)} async-done(((bf16[1,2,512,3,128]{4,1,3,0,2:T(2,128)(2,1)}), bf16[1,2,512,3,128]{4,1,3,0,2:T(2,128)(2,1)S(1)}, u32[]{:S(2)}, u32[]{:S(2)}) %all-to-all-start.1) | async-done | bytes 786464 | tf_op jit(solution)/shard_map/all_to_all | solution.py:135
  283.4 7.9 %fusion.48 = (f32[128]{0:T(128)S(1)}, f32[128,3072]{1,0:T(8,128)S(1)}) fusion(bf16[128,3072]{1,0:T(8,128)(2,1)S(1)} %reshape.60, bf16[3072,3072]{1,0:T(8,128)(2,1)} %param.20, f32[3072]{0:T(1024)S(1)} %bitcast.144, bf16[128,3072]{1,0:T(8,128)(2,1)S(1)} %bitcast.142), kind=kOutput, calls=%fused_computation.80 | convolution fusion | flops 2417491968 | bytes 22032896 | tf_op jit(solution)/shard_map/dot_general | solution.py:137
  292.4 2.3 collective-permute-start
  295.5 1.9 collective-permute-start.1
  298.2 4.1 %collective-permute-done.1 = bf16[2,64,64]{1,2,0:T(8,128)(2,1)S(1)} collective-permute-done((bf16[2,64,64]{1,2,0:T(8,128)(2,1)S(1)}, bf16[2,64,64]{1,2,0:T(8,128)(2,1)S(1)}, u32[]{:S(2)}, u32[]{:S(2)}) %collective-permute-start.1) | collective-permute-done | bytes 16416 | tf_op jit(solution)/shard_map/ppermute | solution.py:32
  (97 shorter events, 37.9 us)
Async XLA Ops:
  7.2 44.1 %copy-start = (bf16[1,256,2,24,128]{4,3,2,1,0:T(8,128)(2,1)S(1)}, bf16[1,256,2,24,128]{4,3,2,1,0:T(8,128)(2,1)}, u32[]{:S(2)}) copy-start(bf16[1,256,2,24,128]{4,3,2,1,0:T(8,128)(2,1)} %param.16) | copy-start | bytes 9437188
  7.2 173.8 %all-gather.3.cloned.1.call-start = ((), (), s32[]{:S(2)}) async-start(), calls=%async_computation.2 | async-start | bytes 14155776 | tf_op jit(solution)/shard_map/all_gather | solution.py:132
  48.5 1.4 copy-start.2
  49.9 2.4 copy-start.10
  259.1 9.7 %copy-start.6 = (f32[1,2,3072]{2,1,0:T(2,128)S(1)}, f32[1,2,3072]{2,1,0:T(2,128)}, u32[]{:S(2)}) copy-start(f32[1,2,3072]{2,1,0:T(2,128)} %param.21) | copy-start | bytes 73732
  262.7 20.7 %copy-start.3 = (bf16[1,2,64,3072]{3,2,1,0:T(8,128)(2,1)S(1)}, bf16[1,2,64,3072]{3,2,1,0:T(8,128)(2,1)}, u32[]{:S(2)}) copy-start(bf16[1,2,64,3072]{3,2,1,0:T(8,128)(2,1)} %param.15) | copy-start | bytes 2359300
  262.7 20.7 %copy-start.7 = (f32[1,3072]{1,0:T(1,128)S(1)}, f32[1,3072]{1,0:T(1,128)}, u32[]{:S(2)}) copy-start(f32[1,3072]{1,0:T(1,128)} %param.19) | copy-start | bytes 36868
  262.7 19.2 %all-to-all-start.1 = ((bf16[1,2,512,3,128]{4,1,3,0,2:T(2,128)(2,1)}), bf16[1,2,512,3,128]{4,1,3,0,2:T(2,128)(2,1)S(1)}, u32[]{:S(2)}, u32[]{:S(2)}) async-start(bf16[1,2,512,3,128]{4,1,3,0,2:T(2,128)(2,1)} %copy.94), calls=%async_computation.1 | async-start | bytes 1572864 | tf_op jit(solution)/shard_map/all_to_all | solution.py:135
  283.4 8.3 %copy-start.9 = (bf16[3072,64]{0,1:T(8,128)(2,1)S(1)}, bf16[3072,64]{0,1:T(8,128)(2,1)}, u32[]{:S(2)}) copy-start(bf16[3072,64]{0,1:T(8,128)(2,1)} %param.22) | copy-start | bytes 1179652
  291.4 3.3 %copy-start.4 = (f32[2,64,64]{2,1,0:T(8,128)S(1)}, f32[2,64,64]{2,1,0:T(8,128)}, u32[]{:S(2)}) copy-start(f32[2,64,64]{2,1,0:T(8,128)} %param.23) | copy-start | bytes 98308
  291.4 11.0 %copy-start.5 = (bf16[3,16,512]{2,1,0:T(8,128)(2,1)S(1)}, bf16[3,16,512]{2,1,0:T(8,128)(2,1)}, u32[]{:S(2)}) copy-start(bf16[3,16,512]{2,1,0:T(8,128)(2,1)} %param.24) | copy-start | bytes 147460
  291.4 11.0 %copy-start.8 = (f32[512]{0:T(512)S(1)}, f32[512]{0:T(512)}, u32[]{:S(2)}) copy-start(f32[512]{0:T(512)} %param.25) | copy-start | bytes 6148
  291.4 12.7 %copy-start.1 = (bf16[1,256,2,24,128]{4,3,2,1,0:T(8,128)(2,1)S(1)}, bf16[1,256,2,24,128]{4,3,2,1,0:T(8,128)(2,1)}, u32[]{:S(2)}) copy-start(bf16[1,256,2,24,128]{4,3,2,1,0:T(8,128)(2,1)} %param.16) | copy-start | bytes 9437188
  292.4 3.1 %collective-permute-start = (bf16[2,64,64]{1,2,0:T(8,128)(2,1)S(1)}, bf16[2,64,64]{1,2,0:T(8,128)(2,1)S(1)}, u32[]{:S(2)}, u32[]{:S(2)}) collective-permute-start(bf16[2,64,64]{1,2,0:T(8,128)(2,1)S(1)} %copy.126), channel_id=1, source_target_pairs={{0,64},{64,0},{1,65},{65,1},{2,66},{66,2},{3,67},{67,3},{4,68},{68... | collective-permute-start | bytes 49160 | tf_op jit(solution)/shard_map/ppermute | solution.py:26
  295.5 6.8 %collective-permute-start.1 = (bf16[2,64,64]{1,2,0:T(8,128)(2,1)S(1)}, bf16[2,64,64]{1,2,0:T(8,128)(2,1)S(1)}, u32[]{:S(2)}, u32[]{:S(2)}) collective-permute-start(bf16[2,64,64]{1,2,0:T(8,128)(2,1)S(1)} %get-tuple-element.85), channel_id=1, source_target_pairs={{0,8},{8,16},{16,24},{24,32},{32,40},{40,48},{48,56},{1,9},{9,17},... | collective-permute-start | bytes 49160 | tf_op jit(solution)/shard_map/ppermute | solution.py:32
Sparse Core Ops, SparseCore 0:
  51.3 129.5 all-gather.2
where the time goes:
time: 312 us; the launch traced here: 311 us
  waiting for transfers between devices  143 us (46%)
  matrix products  47.1 us (15%)
  local copies, waits for them, and re-layouts  38.2 us (12%)
  blocking collectives  37 us (12%)
  other arithmetic  20.2 us (6%)
  between operations  15 us (5%)
  starting transfers between devices  10.3 us (3%)
    all_gather x1, waiting for transfers between devices, shards(): lax.all_gather(heads_view[0, :, :, 1:3], 'blk', axis=0, tiled=True)  125 us
    all_to_all x1, blocking collectives, shards(): lax.all_to_all(qkv_grid, 'sp', split_axis=4, concat_axis=2, tiled=True)  37 us
    dot_general x9, matrix products, fold_block(): jnp.einsum('hqk,khd->qhd', weights.astype(jnp.bfloat16), block_values, pr...  22.8 us
    reduce_sum x9, other arithmetic, fold_block(): new_sum = old_sum * factor + jnp.sum(weights, axis=-1)  17.6 us
    dot_general x9, matrix products, fold_block(): jnp.einsum('qhd,khd->hqk', queries, block_keys, preferred_element_type=jn...  15.1 us
    all_to_all x1, waiting for transfers between devices, shards(): lax.all_to_all(attended, 'sp', split_axis=2, concat_axis=3, tiled=True)  13.1 us
    squeeze x8, local copies, waits for them, and re-layouts, visit(): result, unused = lax.scan(step_block, running, blocks)  12.1 us
    all_gather x1, local copies, waits for them, and re-layouts, shards(): lax.all_gather(heads_view[0, :, :, 1:3], 'blk', axis=0, tiled=True)  10.6 us
  transfers between devices with their start and end apart: 4, of which 4 were waited for; matrix products, arithmetic and copies ran while one was open for 2% of the time, Pallas kernels for 0%

commit v1 on v0

v1 whole, which is shorter than its diff:
```python
import functools
import math

import jax
import jax.numpy as jnp
from jax import lax
from jax.experimental import pallas as pl
from jax.experimental.pallas import tpu as pltpu
from jax.sharding import PartitionSpec as P

D = 3072
H = 24
HD = 128
G = 3
TXT = 256
ROWS = 128
QB = 256
MESH = pl.DeviceIdType.MESH
SCALE = math.log2(math.e) / math.sqrt(HD)
BF = jnp.bfloat16
F32 = jnp.float32

guidance_scale = 6.0
sigma_last = 0.125
vae_factor = 0.476986
norm_eps = 1e-06


def wait_bytes(ref, sem):
    pltpu.make_async_copy(ref, ref, sem).wait()


def body(
    qkv, residual, text, bias, gate, w_out, fmod, w_fin, noisy, conv_w, conv_b,
    velocity, decoded,
    qb, kv, ob, att, tb, mb, wo, res, wf, proj, mod, pb, lat, halo, acc, m_s, l_s,
    snd, rcv_q, rcv_k, rcv_v, ysnd, yrcv, dsnd, drcv, osnd, orcv, lsem, tsnd, trcv, psnd, prcv, hsnd, hrcv,
):
    c = lax.axis_index("cfg")
    b = lax.axis_index("blk")
    s = lax.axis_index("sp")
    xl = b // 4
    y = b % 4
    up = (y + 1) % 4
    dn = (y + 3) % 4
    opp = (y + 2) % 4
    to_up = (c, xl * 4 + up, s)
    to_dn = (c, xl * 4 + dn, s)
    to_core = (1 - c, b, s)
    moved = c != xl

    def peer(d):
        return (xl, c * 4 + y, d)

    def remote(src, dst, send, recv, dev):
        return pltpu.make_async_remote_copy(src, dst, send, recv, device_id=dev, device_id_type=MESH)

    fetch_w = pltpu.make_async_copy(w_out, wo, lsem.at[0])
    fetch_r = pltpu.make_async_copy(residual.at[0], res, lsem.at[1])
    fetch_f = pltpu.make_async_copy(w_fin, wf, lsem.at[2])

    bar = pltpu.get_barrier_semaphore()

    def sig(dev):
        pl.semaphore_signal(bar, inc=1, device_id=dev, device_id_type=MESH)

    sig(to_up)
    sig(to_dn)
    sig(to_core)
    for j in range(1, 8):
        sig(peer((s + j) % 8))

    @pl.when(moved)
    def _():
        sig(peer(s))

    @pl.when(b < 7)
    def _():
        sig((c, b + 1, s))

    @pl.when(b > 0)
    def _():
        sig((c, b - 1, s))

    count = 10 + jnp.where(moved, 1, 0) + jnp.where(b < 7, 1, 0) + jnp.where(b > 0, 1, 0)
    pl.semaphore_wait(bar, count)

    rcvs = (rcv_q, rcv_k, rcv_v)

    def send_head(h):
        for kind in (1, 2, 0):
            landing = qb.at[h, s] if kind == 0 else kv.at[h, y, xl, kind - 1, s]

            def piece(d):
                return qkv.at[0, :, :, pl.ds(pl.multiple_of(kind * D + (d * G + h) * HD, HD), HD)]

            def one(j, carry):
                d = (s + j) % 8
                remote(piece(d), landing, snd.at[h, kind], rcvs[kind].at[h], peer(d)).start()
                return carry

            lax.fori_loop(1, 8, one, 0)

            @pl.when(moved)
            def _():
                remote(piece(s), landing, snd.at[h, kind], rcvs[kind].at[h], peer(s)).start()

            @pl.when(jnp.logical_not(moved))
            def _():
                pltpu.make_async_copy(piece(s), landing, rcvs[kind].at[h]).start()

    def wait_head(h):
        wait_bytes(kv.at[h, y, c, 0], rcv_k.at[h])
        wait_bytes(kv.at[h, y, c, 1], rcv_v.at[h])
        wait_bytes(qb.at[h], rcv_q.at[h])

    def core_copy(h, i, yy):
        return remote(kv.at[h, yy, c], kv.at[h, yy, c], dsnd.at[h, i], drcv.at[h, i], to_core)

    def wait_core(h, i, yy):
        wait_bytes(kv.at[h, yy, 1 - c], drcv.at[h, i])

    def ring_copy(h, i, yy, part, dev):
        ref = kv.at[h, yy, c, part]
        return remote(ref, ref, ysnd.at[h, i], yrcv.at[h, i], dev)

    def wait_ring(h, i, yy, part):
        wait_bytes(kv.at[h, yy, c, part], yrcv.at[h, i])

    def send_own(h):
        ring_copy(h, 0, y, 0, to_up).start()
        ring_copy(h, 2, y, 1, to_dn).start()
        ring_copy(h, 1, y, 1, to_up).start()
        ring_copy(h, 3, y, 0, to_dn).start()
        core_copy(h, 0, y).start()

    text_own = pltpu.make_async_copy(text, tb.at[c], lsem.at[3])
    text_out = remote(text, tb.at[c], tsnd.at[0], trcv.at[0], to_core)
    mask_own = pltpu.make_async_copy(bias, mb.at[c], lsem.at[4])
    mask_out = remote(bias, mb.at[c], tsnd.at[1], trcv.at[1], to_core)

    send_head(0)
    text_own.start()
    text_out.start()
    mask_own.start()
    mask_out.start()
    send_head(1)
    send_head(2)
    fetch_w.start()
    fetch_r.start()
    fetch_f.start()

    text_own.wait()
    mask_own.wait()
    wait_bytes(tb.at[1 - c], trcv.at[0])
    wait_bytes(mb.at[1 - c], trcv.at[1])

    wait_head(0)
    send_own(0)

    def queries(h, u):
        return qb[h, pl.ds(2 * u, 2)].reshape(QB, HD)

    def scores(q, keys):
        return lax.dot_general(q, keys, (((1,), (1,)), ((), ())), preferred_element_type=F32)

    def weigh(weights, values):
        padded = jnp.concatenate([values, jnp.ones_like(values)], axis=1)
        return jnp.dot(weights.astype(BF), padded, preferred_element_type=F32)

    blocks = 1024 // QB

    def text_step(h):
        keys = tb[xl, h, 0]
        values = tb[xl, h, 1]
        added = mb[xl]
        for u in range(blocks):
            rows = pl.ds(u * QB, QB)
            sc = scores(queries(h, u), keys) + added[0:1]
            top = jnp.max(sc, axis=1, keepdims=True)
            out = weigh(jnp.exp2((sc - top) * SCALE), values)
            m_s[rows] = jnp.broadcast_to(top, (QB, HD))
            acc[rows] = out[:, :HD]
            l_s[rows] = out[:, HD:]

    def key_step(h, yy):
        keys = kv[h, yy, :, 0].reshape(2048, HD)
        values = kv[h, yy, :, 1].reshape(2048, HD)

        def finish(u, sc):
            rows = pl.ds(u * QB, QB)
            old = m_s[rows]
            new = jnp.maximum(old, jnp.max(sc, axis=1, keepdims=True))
            factor = jnp.exp2((old - new) * SCALE)
            out = weigh(jnp.exp2((sc - new[:, :1]) * SCALE), values)
            m_s[rows] = new
            acc[rows] = acc[rows] * factor + out[:, :HD]
            l_s[rows] = l_s[rows] * factor + out[:, HD:]

        now = scores(queries(h, 0), keys)
        for u in range(blocks):
            later = scores(queries(h, u + 1), keys) if u + 1 < blocks else None
            finish(u, now)
            now = later

    def project(h, first):
        wait_bytes(att.at[:, h], orcv.at[h])
        rows = jnp.concatenate([att[d, h].reshape(ROWS, HD) for d in range(8)], axis=1)

        def columns(n, carry):
            cols = pl.ds(pl.multiple_of(n * 512, 512), 512)
            weight = jnp.concatenate(
                [wo[pl.ds(pl.multiple_of((d * G + h) * HD, HD), HD), cols] for d in range(8)], axis=0
            )
            out = jnp.dot(rows, weight, preferred_element_type=F32)
            if first:
                proj[:, cols] = out
            else:
                proj[:, cols] += out
            return carry

        lax.fori_loop(0, D // 512, columns, 0)

    def send_back(h):
        ob[h] = (acc[...] / l_s[...]).astype(BF).reshape(8, 2, 64, HD)

        def one(j, carry):
            d = (s + j) % 8
            remote(ob.at[h, d], att.at[s, h], osnd.at[h], orcv.at[h], peer(d)).start()
            return carry

        lax.fori_loop(1, 8, one, 0)

        @pl.when(moved)
        def _():
            remote(ob.at[h, s], att.at[s, h], osnd.at[h], orcv.at[h], peer(s)).start()

        @pl.when(jnp.logical_not(moved))
        def _():
            pltpu.make_async_copy(ob.at[h, s], att.at[s, h], orcv.at[h]).start()

    def step(t, carry):
        h = t // 4
        p = t % 4
        yy = (y + p + p // 2 - 2 * (p // 3)) % 4

        @pl.when(p == 0)
        def _():
            text_step(h)

        @pl.when(p == 1)
        def _():
            wait_ring(h, 2, up, 1)
            ring_copy(h, 5, up, 1, to_dn).start()
            wait_ring(h, 0, dn, 0)
            ring_copy(h, 4, dn, 0, to_up).start()
            wait_ring(h, 3, up, 0)
            core_copy(h, 1, up).start()
            wait_ring(h, 1, dn, 1)
            core_copy(h, 2, dn).start()

            @pl.when(h < 2)
            def _():
                wait_head(h + 1)
                send_own(h + 1)

        @pl.when(p == 3)
        def _():
            wait_ring(h, 4, opp, 0)
            wait_ring(h, 5, opp, 1)
            core_copy(h, 3, opp).start()

        wait_core(h, p, yy)
        key_step(h, yy)

        @pl.when(p == 3)
        def _():
            send_back(h)

        @pl.when(t == 6)
        def _():
            fetch_w.wait()
            project(0, True)

        @pl.when(t == 10)
        def _():
            project(1, False)

        return carry

    lax.fori_loop(0, 12, step, 0)
    project(2, False)

    fetch_r.wait()
    fetch_f.wait()

    def norm(n, carry):
        rows = pl.ds(pl.multiple_of(n * 32, 32), 32)
        shown = res[n // 2, pl.ds(pl.multiple_of((n % 2) * 32, 32), 32)].astype(F32)
        hidden = shown + gate[...] * proj[rows]
        centered = hidden - jnp.mean(hidden, axis=1, keepdims=True)
        normed = centered * lax.rsqrt(jnp.mean(centered * centered, axis=1, keepdims=True) + norm_eps)
        mod[rows] = (normed * (1.0 + fmod[0, 1:2]) + fmod[0, 0:1]).astype(BF)
        return carry

    lax.fori_loop(0, 4, norm, 0)
    pb[c] = jnp.dot(mod[...], wf[...], preferred_element_type=F32)
    pred_out = remote(pb.at[c], pb.at[c], psnd, prcv, to_core)
    pred_out.start()
    wait_bytes(pb.at[1 - c], prcv)
    uncond = pb[1]
    guided = uncond + guidance_scale * (pb[0] - uncond)
    velocity[...] = guided
    lat[...] = ((noisy[...] - sigma_last * guided) / vae_factor).astype(BF)

    @pl.when(b < 7)
    def _():
        remote(lat, halo, hsnd, hrcv, (c, b + 1, s)).start()

    @pl.when(b == 0)
    def _():
        halo[...] = jnp.zeros_like(halo)

    @pl.when(b > 0)
    def _():
        wait_bytes(halo, hrcv)

    before = halo[...]
    here = lat[...]
    across = jnp.concatenate([before[64:], here[:64]], axis=0)
    entry = lax.broadcasted_iota(jnp.int32, (64, 48), 0)
    place = lax.broadcasted_iota(jnp.int32, (64, 48), 1)
    for i in range(2):
        taps = jnp.zeros((ROWS, 48), F32)
        for t, frames in enumerate((before, across, here)):
            chosen = (entry == 4 * (place - 16 * t) + 2 * c + i) & (place >= 16 * t) & (place < 16 * t + 16)
            taps = taps + jnp.dot(frames, jnp.where(chosen, 1.0, 0.0).astype(BF), preferred_element_type=F32)
        out = jnp.dot(taps.astype(BF), conv_w[...], preferred_element_type=F32) + conv_b[...]
        decoded[:, i * 512 : (i + 1) * 512] = out.astype(BF)

    for h in range(3):
        for kind in range(3):
            wait_bytes(qb.at[h, pl.ds(0, 7)], snd.at[h, kind])

            @pl.when(moved)
            def _():
                wait_bytes(qb.at[h, 0], snd.at[h, kind])

        for i in range(6):
            wait_bytes(kv.at[h, y, c, 0], ysnd.at[h, i])
        for i in range(4):
            wait_bytes(kv.at[h, y, c], dsnd.at[h, i])
        wait_bytes(ob.at[h, pl.ds(0, 7)], osnd.at[h])

        @pl.when(moved)
        def _():
            wait_bytes(ob.at[h, 0], osnd.at[h])

    wait_bytes(tb.at[c], tsnd.at[0])
    wait_bytes(mb.at[c], tsnd.at[1])
    wait_bytes(pb.at[c], psnd)

    @pl.when(b < 7)
    def _():
        wait_bytes(lat, hsnd)


def shards(qkv, residual, text_kv, text_len, text_keep, attn_gate, w_out, final_mod, w_final, noisy, conv_weight, conv_bias):
    text_mask = (jnp.arange(TXT, dtype=jnp.int32) < text_len[0]) & (text_keep[0] == 1)
    bias = jnp.broadcast_to(jnp.where(text_mask, 0.0, -1e30).astype(F32)[None], (8, TXT))
    text = lax.dynamic_slice_in_dim(text_kv[0], lax.axis_index("sp") * G, G, axis=2)
    text = jnp.transpose(text, (2, 1, 0, 3))
    hbm = pl.BlockSpec(memory_space=pl.ANY)
    vmem = pl.BlockSpec(memory_space=pltpu.VMEM)
    dma = pltpu.SemaphoreType.DMA
    velocity, decoded = pl.pallas_call(
        body,
        out_shape=(
            jax.ShapeDtypeStruct((ROWS, 64), F32),
            jax.ShapeDtypeStruct((ROWS, 1024), BF),
        ),
        in_specs=[hbm, hbm, vmem, vmem, vmem, hbm, vmem, hbm, vmem, vmem, vmem],
        out_specs=(vmem, vmem),
        scratch_shapes=[
            pltpu.VMEM((G, 8, 2, 64, HD), BF),
            pltpu.VMEM((G, 4, 2, 2, 8, 2, 64, HD), BF),
            pltpu.VMEM((G, 8, 2, 64, HD), BF),
            pltpu.VMEM((8, G, 2, 64, HD), BF),
            pltpu.VMEM((2, G, 2, TXT, HD), BF),
            pltpu.VMEM((2, 8, TXT), F32),
            pltpu.VMEM((D, D), BF),
            pltpu.VMEM((2, 64, D), BF),
            pltpu.VMEM((D, 64), BF),
            pltpu.VMEM((ROWS, D), F32),
            pltpu.VMEM((ROWS, D), BF),
            pltpu.VMEM((2, ROWS, 64), F32),
            pltpu.VMEM((ROWS, 64), BF),
            pltpu.VMEM((ROWS, 64), BF),
            pltpu.VMEM((1024, HD), F32),
            pltpu.VMEM((1024, HD), F32),
            pltpu.VMEM((1024, HD), F32),
            dma((G, 3)),
            dma((G,)),
            dma((G,)),
            dma((G,)),
            dma((G, 6)),
            dma((G, 6)),
            dma((G, 4)),
            dma((G, 4)),
            dma((G,)),
            dma((G,)),
            dma((5,)),
            dma((2,)),
            dma((2,)),
            dma,
            dma,
            dma,
            dma,
        ],
        compiler_params=pltpu.CompilerParams(
            collective_id=0, has_side_effects=True, vmem_limit_bytes=60 * 2**20
        ),
    )(
        qkv,
        residual,
        text,
        bias,
        attn_gate,
        w_out,
        final_mod,
        w_final,
        noisy.reshape(ROWS, 64),
        conv_weight.reshape(48, 512),
        conv_bias.reshape(1, 512),
    )
    return velocity.reshape(2, 64, 64), decoded.reshape(2, 64, 2, 512)


def solution(mesh):
    return jax.shard_map(
        shards,
        mesh=mesh,
        in_specs=(
            P("cfg", "blk", "sp", None),
            P("cfg", "blk", "sp", None),
            P("cfg", None, None, None, None),
            P("cfg"),
            P("cfg", None),
            P("cfg", None),
            P(),
            P("cfg", None, None),
            P(),
            P("blk", "sp", None),
            P(),
            P(),
        ),
        out_specs=(P("blk", "sp", None), P("blk", "sp", "cfg", None)),
        check_vma=False,
    )
```

time: 312 us -> 108 us (0.35)
  waiting for transfers between devices: 143 us -> 0 us
  Pallas kernels: 0 us -> 98.4 us
  matrix products: 47.1 us -> 0 us
  blocking collectives: 37 us -> 0 us
  local copies, waits for them, and re-layouts: 38.2 us -> 7.23 us
  other arithmetic: 20.2 us -> 0.84 us
  between operations: 15 us -> 1.45 us
  starting transfers between devices: 10.3 us -> 0 us
    all_gather x1 -> x0, waiting for transfers between devices: 125 us -> none  [shards(): lax.all_gather(heads_view[0, :, :, 1:3], 'blk', axis=0, tiled=True)]
    pallas_call x0 -> x1, Pallas kernels: none -> 98.4 us  [shards(): pl.pallas_call(body, out_shape=(jax.ShapeDtypeStruct((ROWS, 64), F32), ja...]
    dot_general x23 -> x0, matrix products: 47.1 us -> none  [the longest x9 22.8 us: fold_block(): jnp.einsum('hqk,khd->qhd', weights.astype(jnp.bfloat16), block_values, pr...]
    all_to_all x1 -> x0, blocking collectives: 37 us -> none  [shards(): lax.all_to_all(qkv_grid, 'sp', split_axis=4, concat_axis=2, tiled=True)]
    reduce_sum x10 -> x0, other arithmetic: 17.9 us -> none  [the longest x9 17.6 us: fold_block(): new_sum = old_sum * factor + jnp.sum(weights, axis=-1)]
    all_to_all x1 -> x0, waiting for transfers between devices: 13.1 us -> none  [shards(): lax.all_to_all(attended, 'sp', split_axis=2, concat_axis=3, tiled=True)]
    squeeze x8 -> x0, local copies, waits for them, and re-layouts: 12.1 us -> none  [visit(): result, unused = lax.scan(step_block, running, blocks)]
    all_gather x1 -> x0, local copies, waits for them, and re-layouts: 10.6 us -> none  [shards(): lax.all_gather(heads_view[0, :, :, 1:3], 'blk', axis=0, tiled=True)]
  transfers between devices with their start and end apart: 4 -> 0, of which waited for: 4 -> 0; matrix products, arithmetic and copies ran while one was open for 2% -> 0% of each run, Pallas kernels for 0% -> 0%
where the time goes in v1:
time: 108 us
  Pallas kernels  98.4 us (91%)
  local copies, waits for them, and re-layouts  7.23 us (7%)
  between operations  1.45 us (1%)
    pallas_call x1, Pallas kernels, shards(): pl.pallas_call(body, out_shape=(jax.ShapeDtypeStruct((ROWS, 64), F32), ja...  98.4 us
    unnamed x4, local copies, waits for them, and re-layouts  3.63 us

profile of v1, /device:TPU:3, one launch (start us, length us, event | category | flops | bytes accessed | tf_op | source)
XLA Modules:
  0.0 108.0 jit_solution(16449629458457893979)
XLA Ops:
  0.6 0.0 copy-start
  1.4 0.8 and_select_fusion
  2.3 0.6 broadcast_in_dim.19.bias
  2.9 0.0 copy-done
  2.9 0.3 constant_dynamic-slice_fusion
  3.2 0.8 copy.17
  4.0 2.2 %copy.15.w_fin = bf16[3072,64]{1,0:T(8,128)(2,1)} copy(bf16[3072,64]{0,1:T(8,128)(2,1)} %param.20) | data formatting | bytes 786432 | tf_op args[8]
  6.2 98.4 %shard_map.131 = (f32[128,64]{1,0:T(8,128)}, bf16[128,1024]{1,0:T(8,128)(2,1)}) custom-call(bf16[1,2,64,9216]{3,2,1,0:T(8,128)(2,1)} %qkv.1, bf16[1,2,64,3072]{3,2,1,0:T(8,128)(2,1)} %residual.1, bf16[3,2,256,128]{3,2,1,0:T(8,128)(2,1)} %bitcast.12, f32[8,256]{1,0:T(8,128)} %broadcast_in_dim.19.bias, f32[1,3072]{1,0:T(1,128)} %gate.1, ...), custom_call_target="tpu_custom_call" | custom-call | tf_op jit(solution)/shard_map/pallas_call | solution.py:376
  104.6 1.9 %reshape.31 = bf16[2,64,2,512]{3,2,1,0:T(2,128)(2,1)} reshape(bf16[128,1024]{1,0:T(8,128)(2,1)} %get-tuple-element.5) | data formatting | bytes 524288 | tf_op jit(solution)/shard_map/reshape | solution.py:436
  106.5 1.5 %copy.20 = f32[2,64,64]{2,1,0:T(8,128)} copy(f32[2,64,64]{2,1,0:T(8,128)} %bitcast.14) | data formatting | bytes 65536
Async XLA Ops:
  0.6 2.3 %copy-start = (bf16[1,256,2,24,128]{4,3,2,1,0:T(8,128)(2,1)S(1)}, bf16[1,256,2,24,128]{4,3,2,1,0:T(8,128)(2,1)}, u32[]{:S(2)}) copy-start(bf16[1,256,2,24,128]{4,3,2,1,0:T(8,128)(2,1)} %param.14) | copy-start | bytes 9437188

commit v2 on v1

v2 whole, which is shorter than its diff:
```python
import functools
import math

import jax
import jax.numpy as jnp
from jax import lax
from jax.experimental import pallas as pl
from jax.experimental.pallas import tpu as pltpu
from jax.sharding import PartitionSpec as P

D = 3072
H = 24
HD = 128
G = 3
TXT = 256
ROWS = 128
QB = 256
MESH = pl.DeviceIdType.MESH
SCALE = math.log2(math.e) / math.sqrt(HD)
BF = jnp.bfloat16
F32 = jnp.float32

guidance_scale = 6.0
sigma_last = 0.125
vae_factor = 0.476986
norm_eps = 1e-06


def wait_bytes(ref, sem):
    pltpu.make_async_copy(ref, ref, sem).wait()


def body(
    qkv, residual, text, tlen, keep, gate, w_out, fmod, w_fin, noisy,
    guided_out, latents,
    qb, kv, ob, att, po, pr, so, sr, tb, mo, mb, wo, res, wf, proj, mod, pb, lat, halo, acc, m_s, l_s,
    snd, rcv_q, rcv_k, rcv_v, ysnd, yrcv, dsnd, drcv, psnd, prcv, osnd, orcv, lsem, tsnd, trcv, gsnd, grcv, hsnd, hrcv,
):
    c = lax.axis_index("cfg")
    b = lax.axis_index("blk")
    s = lax.axis_index("sp")
    xl = b // 4
    y = b % 4
    to_q = (c, xl * 4 + y + 1 - 2 * (y % 2), s)
    to_k = (c, xl * 4 + 3 - y, s)
    to_core = (1 - c, b, s)
    moved = c != xl

    def peer(d):
        return (xl, c * 4 + y, d)

    def remote(src, dst, send, recv, dev):
        return pltpu.make_async_remote_copy(src, dst, send, recv, device_id=dev, device_id_type=MESH)

    fetch_w = pltpu.make_async_copy(w_out, wo, lsem.at[0])
    fetch_r = pltpu.make_async_copy(residual.at[0], res, lsem.at[1])
    fetch_f = pltpu.make_async_copy(w_fin, wf, lsem.at[2])

    bar = pltpu.get_barrier_semaphore()

    def sig(dev):
        pl.semaphore_signal(bar, inc=1, device_id=dev, device_id_type=MESH)

    sig(to_q)
    sig(to_k)
    sig(to_core)
    for j in range(1, 8):
        sig(peer((s + j) % 8))

    @pl.when(moved)
    def _():
        sig(peer(s))

    @pl.when(b < 7)
    def _():
        sig((c, b + 1, s))

    @pl.when(b > 0)
    def _():
        sig((c, b - 1, s))

    kept = (lax.broadcasted_iota(jnp.int32, (1, TXT), 1) < tlen[0]) & (keep[...] == 1)
    mo[...] = jnp.broadcast_to(jnp.where(kept, 0.0, -1e30).astype(F32), (8, TXT))

    count = 10 + jnp.where(moved, 1, 0) + jnp.where(b < 7, 1, 0) + jnp.where(b > 0, 1, 0)
    pl.semaphore_wait(bar, count)

    rcvs = (rcv_q, rcv_k, rcv_v)

    def send_head(h):
        for kind in (1, 2, 0):
            landing = qb.at[h, 0, s] if kind == 0 else kv.at[h, 0, xl, kind - 1, s]

            def piece(d):
                return qkv.at[0, :, :, pl.ds(pl.multiple_of(kind * D + (d * G + h) * HD, HD), HD)]

            def one(j, carry):
                d = (s + j) % 8
                remote(piece(d), landing, snd.at[h, kind], rcvs[kind].at[h], peer(d)).start()
                return carry

            lax.fori_loop(1, 8, one, 0)

            @pl.when(moved)
            def _():
                remote(piece(s), landing, snd.at[h, kind], rcvs[kind].at[h], peer(s)).start()

            @pl.when(jnp.logical_not(moved))
            def _():
                pltpu.make_async_copy(piece(s), landing, rcvs[kind].at[h]).start()

    def share_head(h):
        for kind in range(2):
            wait_bytes(kv.at[h, 0, c, kind], (rcv_k, rcv_v)[kind].at[h])
            mine = kv.at[h, 0, c, kind]
            remote(mine, kv.at[h, 1, c, kind], ysnd.at[h, kind], yrcv.at[h, kind], to_k).start()
            remote(mine, mine, dsnd.at[h, 0, kind], drcv.at[h, 0, kind], to_core).start()
        wait_bytes(qb.at[h, 0], rcv_q.at[h])
        remote(qb.at[h, 0], qb.at[h, 1], ysnd.at[h, 2], yrcv.at[h, 2], to_q).start()

    def pass_far(h):
        for kind in range(2):
            far = kv.at[h, 1, c, kind]
            wait_bytes(far, yrcv.at[h, kind])
            remote(far, far, dsnd.at[h, 1, kind], drcv.at[h, 1, kind], to_core).start()

    def wait_core(h, far):
        for kind in range(2):
            wait_bytes(kv.at[h, far, 1 - c, kind], drcv.at[h, far, kind])

    text_own = pltpu.make_async_copy(text, tb.at[c], lsem.at[3])
    text_out = remote(text, tb.at[c], tsnd.at[0], trcv.at[0], to_core)
    mask_own = pltpu.make_async_copy(mo, mb.at[c], lsem.at[4])
    mask_out = remote(mo, mb.at[c], tsnd.at[1], trcv.at[1], to_core)

    send_head(0)
    text_own.start()
    text_out.start()
    mask_own.start()
    mask_out.start()
    send_head(1)
    send_head(2)
    fetch_w.start()
    fetch_r.start()
    fetch_f.start()

    text_own.wait()
    mask_own.wait()
    wait_bytes(tb.at[1 - c], trcv.at[0])
    wait_bytes(mb.at[1 - c], trcv.at[1])

    def queries(h, r, u):
        return qb[h, r, pl.ds(2 * u, 2)].reshape(QB, HD)

    def scores(q, keys):
        return lax.dot_general(q, keys, (((1,), (1,)), ((), ())), preferred_element_type=F32)

    def weigh(weights, values):
        padded = jnp.concatenate([values, jnp.ones_like(values)], axis=1)
        return jnp.dot(weights.astype(BF), padded, preferred_element_type=F32)

    blocks = 1024 // QB

    def text_step(h):
        keys = tb[xl, h, 0]
        values = tb[xl, h, 1]
        added = mb[xl]
        par = h % 2
        for u in range(blocks):
            rows = pl.ds(u * QB, QB)
            sc = scores(queries(h, 0, u), keys) + added[0:1]
            top = jnp.max(sc, axis=1, keepdims=True)
            out = weigh(jnp.exp2((sc - top) * SCALE), values)
            m_s[par, 0, rows] = jnp.broadcast_to(top, (QB, HD))
            acc[par, 0, rows] = out[:, :HD]
            l_s[par, 0, rows] = out[:, HD:]

    def softmax_blocks(h, far, rowsets, done):
        keys = kv[h, far, :, 0].reshape(2048, HD)
        values = kv[h, far, :, 1].reshape(2048, HD)
        par = h % 2
        order = [(r, u) for r in rowsets for u in range(blocks)]
        now = scores(queries(h, *order[0]), keys)
        for i, (r, u) in enumerate(order):
            later = scores(queries(h, *order[i + 1]), keys) if i + 1 < len(order) else None
            rows = pl.ds(u * QB, QB)
            top = jnp.max(now, axis=1, keepdims=True)
            if far == 0 and r == 1:
                new = jnp.broadcast_to(top, (QB, HD))
                out = weigh(jnp.exp2((now - top) * SCALE), values)
                total, weight = out[:, :HD], out[:, HD:]
            else:
                old = m_s[par, r, rows]
                new = jnp.maximum(old, top)
                factor = jnp.exp2((old - new) * SCALE)
                out = weigh(jnp.exp2((now - new[:, :1]) * SCALE), values)
                total = acc[par, r, rows] * factor + out[:, :HD]
                weight = l_s[par, r, rows] * factor + out[:, HD:]
            if r == 1 and far == 1:
                done(u, new, total, weight)
            else:
                m_s[par, r, rows] = new
                acc[par, r, rows] = total
                l_s[par, r, rows] = weight
            now = later

    def far_step(h):
        def done(u, top, total, weight):
            cols = pl.ds(u * QB, QB)
            po[h, pl.ds(2 * u, 2)] = (total / weight).astype(BF).reshape(2, 2, 64, HD)
            lane = lax.broadcasted_iota(jnp.int32, (QB, HD), 1)
            so[h, :, cols] = jnp.where(lane == 0, top, weight).T[0:8]
            part = po.at[h, pl.ds(2 * u, 2)]
            remote(part, pr.at[h, pl.ds(2 * u, 2)], psnd.at[h, 0], prcv.at[h, 0], to_q).start()
            remote(so.at[h, :, cols], sr.at[h, :, cols], psnd.at[h, 1], prcv.at[h, 1], to_q).start()

        softmax_blocks(h, 1, (1, 0), done)

    def join(h):
        wait_bytes(pr.at[h], prcv.at[h, 0])
        wait_bytes(sr.at[h], prcv.at[h, 1])
        par = h % 2

        def block(j, carry):
            u = (j + s // 2) % blocks
            rows = pl.ds(pl.multiple_of(u * QB, QB), QB)
            stats = sr[h, :, rows].T
            top_p = stats[:, 0:1]
            sum_p = stats[:, 1:2]
            top_a = m_s[par, 0, rows]
            new = jnp.maximum(top_a, top_p)
            f_a = jnp.exp2((top_a - new) * SCALE)
            f_p = jnp.exp2((top_p - new) * SCALE) * sum_p
            partial = pr[h, pl.ds(2 * u, 2)].reshape(QB, HD).astype(F32)
            out = (acc[par, 0, rows] * f_a + partial * f_p) / (l_s[par, 0, rows] * f_a + f_p)
            ob[h, pl.ds(2 * u, 2)] = out.astype(BF).reshape(2, 2, 64, HD)
            for k in range(2):
                d = 2 * u + k

                @pl.when(jnp.logical_or(moved, d != s))
                def _():
                    remote(ob.at[h, d], att.at[s, h], osnd.at[h], orcv.at[h], peer(d)).start()

                @pl.when(jnp.logical_not(jnp.logical_or(moved, d != s)))
                def _():
                    pltpu.make_async_copy(ob.at[h, d], att.at[s, h], orcv.at[h]).start()

            return carry

        lax.fori_loop(0, blocks, block, 0)

    def project(h):
        wait_bytes(att.at[:, h], orcv.at[h])
        rows = jnp.concatenate([att[d, h].reshape(ROWS, HD) for d in range(8)], axis=1)

        def columns(n, carry):
            cols = pl.ds(pl.multiple_of(n * 512, 512), 512)
            weight = jnp.concatenate(
                [wo[pl.ds(pl.multiple_of((d * G + h) * HD, HD), HD), cols] for d in range(8)], axis=0
            )
            proj[:, cols] += jnp.dot(rows, weight, preferred_element_type=F32)
            return carry

        lax.fori_loop(0, D // 512, columns, 0)

    proj[...] = jnp.zeros_like(proj)
    share_head(0)
    wait_core(0, 0)
    text_step(0)
    softmax_blocks(0, 0, (0,), None)
    wait_bytes(qb.at[0, 1], yrcv.at[0, 2])
    softmax_blocks(0, 0, (1,), None)

    def step(h, carry):
        @pl.when(h < 2)
        def _():
            share_head(h + 1)

        pass_far(h)

        @pl.when(h < 2)
        def _():
            wait_core(h + 1, 0)
            text_step(h + 1)
            softmax_blocks(h + 1, 0, (0,), None)

        @pl.when(h == 1)
        def _():
            fetch_w.wait()

        @pl.when(h > 0)
        def _():
            project(h - 1)

        wait_core(h, 1)
        far_step(h)

        @pl.when(h < 2)
        def _():
            wait_bytes(qb.at[h + 1, 1], yrcv.at[h + 1, 2])
            softmax_blocks(h + 1, 0, (1,), None)

        join(h)
        return carry

    lax.fori_loop(0, G, step, 0)
    project(G - 1)

    fetch_r.wait()
    fetch_f.wait()

    def norm(n, carry):
        rows = pl.ds(pl.multiple_of(n * 32, 32), 32)
        shown = res[n // 2, pl.ds(pl.multiple_of((n % 2) * 32, 32), 32)].astype(F32)
        hidden = shown + gate[...] * proj[rows]
        centered = hidden - jnp.mean(hidden, axis=1, keepdims=True)
        normed = centered * lax.rsqrt(jnp.mean(centered * centered, axis=1, keepdims=True) + norm_eps)
        mod[rows] = (normed * (1.0 + fmod[0, 1:2]) + fmod[0, 0:1]).astype(BF)
        return carry

    lax.fori_loop(0, 4, norm, 0)
    pb[c] = lax.dot_general(mod[...], wf[...], (((1,), (1,)), ((), ())), preferred_element_type=F32)
    remote(pb.at[c], pb.at[c], gsnd, grcv, to_core).start()
    wait_bytes(pb.at[1 - c], grcv)
    uncond = pb[1]
    guided = uncond + guidance_scale * (pb[0] - uncond)
    guided_out[...] = guided
    lat[...] = ((noisy[...] - sigma_last * guided) / vae_factor).astype(BF)

    @pl.when(b < 7)
    def _():
        remote(lat, halo, hsnd, hrcv, (c, b + 1, s)).start()

    latents[1] = lat[...]

    @pl.when(b == 0)
    def _():
        latents[0] = jnp.zeros_like(halo)

    @pl.when(b > 0)
    def _():
        wait_bytes(halo, hrcv)
        latents[0] = halo[...]

    for h in range(G):
        for kind in range(3):
            wait_bytes(qb.at[h, 0, pl.ds(0, 7)], snd.at[h, kind])

            @pl.when(moved)
            def _():
                wait_bytes(qb.at[h, 0, 0], snd.at[h, kind])

            wait_bytes(kv.at[h, 0, c, 0], ysnd.at[h, kind])
        for far in range(2):
            for kind in range(2):
                wait_bytes(kv.at[h, 0, c, 0], dsnd.at[h, far, kind])
        wait_bytes(po.at[h], psnd.at[h, 0])
        wait_bytes(so.at[h], psnd.at[h, 1])
        wait_bytes(ob.at[h, pl.ds(0, 7)], osnd.at[h])

        @pl.when(moved)
        def _():
            wait_bytes(ob.at[h, 0], osnd.at[h])

    wait_bytes(tb.at[c], tsnd.at[0])
    wait_bytes(mb.at[c], tsnd.at[1])
    wait_bytes(pb.at[c], gsnd)

    @pl.when(b < 7)
    def _():
        wait_bytes(lat, hsnd)


def conv_body(guided, latents, conv_w, conv_b, velocity, decoded):
    c = lax.axis_index("cfg")
    velocity[...] = guided[...].reshape(2, 64, 64)
    before = latents[0]
    here = latents[1]
    across = jnp.concatenate([before[64:], here[:64]], axis=0)
    entry = lax.broadcasted_iota(jnp.int32, (64, 48), 0)
    place = lax.broadcasted_iota(jnp.int32, (64, 48), 1)
    outs = []
    for i in range(2):
        taps = jnp.zeros((ROWS, 48), F32)
        for t, frames in enumerate((before, across, here)):
            chosen = (entry == 4 * (place - 16 * t) + 2 * c + i) & (place >= 16 * t) & (place < 16 * t + 16)
            taps = taps + jnp.dot(frames, jnp.where(chosen, 1.0, 0.0).astype(BF), preferred_element_type=F32)
        out = jnp.dot(taps.astype(BF), conv_w[...], preferred_element_type=F32) + conv_b[...]
        outs.append(out.reshape(2, 64, 512))
    decoded[...] = jnp.stack(outs, axis=2).astype(BF)


def shards(qkv, residual, text_kv, text_len, text_keep, attn_gate, w_out, final_mod, w_final, noisy, conv_weight, conv_bias):
    text = lax.dynamic_slice_in_dim(text_kv[0], lax.axis_index("sp") * G, G, axis=2)
    text = jnp.transpose(text, (2, 1, 0, 3))
    hbm = pl.BlockSpec(memory_space=pl.ANY)
    vmem = pl.BlockSpec(memory_space=pltpu.VMEM)
    smem = pl.BlockSpec(memory_space=pltpu.SMEM)
    dma = pltpu.SemaphoreType.DMA
    guided, latents = pl.pallas_call(
        body,
        out_shape=(
            jax.ShapeDtypeStruct((ROWS, 64), F32),
            jax.ShapeDtypeStruct((2, ROWS, 64), BF),
        ),
        in_specs=[hbm, hbm, vmem, smem, vmem, vmem, hbm, vmem, hbm, vmem],
        out_specs=(vmem, vmem),
        scratch_shapes=[
            pltpu.VMEM((G, 2, 8, 2, 64, HD), BF),
            pltpu.VMEM((G, 2, 2, 2, 8, 2, 64, HD), BF),
            pltpu.VMEM((G, 8, 2, 64, HD), BF),
            pltpu.VMEM((8, G, 2, 64, HD), BF),
            pltpu.VMEM((G, 8, 2, 64, HD), BF),
            pltpu.VMEM((G, 8, 2, 64, HD), BF),
            pltpu.VMEM((G, 8, 1024), F32),
            pltpu.VMEM((G, 8, 1024), F32),
            pltpu.VMEM((2, G, 2, TXT, HD), BF),
            pltpu.VMEM((8, TXT), F32),
            pltpu.VMEM((2, 8, TXT), F32),
            pltpu.VMEM((D, D), BF),
            pltpu.VMEM((2, 64, D), BF),
            pltpu.VMEM((64, D), BF),
            pltpu.VMEM((ROWS, D), F32),
            pltpu.VMEM((ROWS, D), BF),
            pltpu.VMEM((2, ROWS, 64), F32),
            pltpu.VMEM((ROWS, 64), BF),
            pltpu.VMEM((ROWS, 64), BF),
            pltpu.VMEM((2, 2, 1024, HD), F32),
            pltpu.VMEM((2, 2, 1024, HD), F32),
            pltpu.VMEM((2, 2, 1024, HD), F32),
            dma((G, 3)),
            dma((G,)),
            dma((G,)),
            dma((G,)),
            dma((G, 3)),
            dma((G, 3)),
            dma((G, 2, 2)),
            dma((G, 2, 2)),
            dma((G, 2)),
            dma((G, 2)),
            dma((G,)),
            dma((G,)),
            dma((5,)),
            dma((2,)),
            dma((2,)),
            dma,
            dma,
            dma,
            dma,
        ],
        compiler_params=pltpu.CompilerParams(
            collective_id=0, has_side_effects=True, vmem_limit_bytes=60 * 2**20
        ),
    )(
        qkv,
        residual,
        text,
        text_len,
        text_keep,
        attn_gate,
        w_out,
        final_mod,
        w_final.T,
        noisy.reshape(ROWS, 64),
    )
    return pl.pallas_call(
        conv_body,
        out_shape=(
            jax.ShapeDtypeStruct((2, 64, 64), F32),
            jax.ShapeDtypeStruct((2, 64, 2, 512), BF),
        ),
        in_specs=[vmem] * 4,
        out_specs=(vmem, vmem),
    )(guided, latents, conv_weight.reshape(48, 512), conv_bias.reshape(1, 512))


def solution(mesh):
    return jax.shard_map(
        shards,
        mesh=mesh,
        in_specs=(
            P("cfg", "blk", "sp", None),
            P("cfg", "blk", "sp", None),
            P("cfg", None, None, None, None),
            P("cfg"),
            P("cfg", None),
            P("cfg", None),
            P(),
            P("cfg", None, None),
            P(),
            P("blk", "sp", None),
            P(),
            P(),
        ),
        out_specs=(P("blk", "sp", None), P("blk", "sp", "cfg", None)),
        check_vma=False,
    )
```

time: 108 us -> 104 us (0.963)
  local copies, waits for them, and re-layouts: 7.23 us -> 3.03 us
  Pallas kernels: 98.4 us -> 99.7 us
    pallas_call x0 -> x1, Pallas kernels: none -> 2.43 us  [shards(): pl.pallas_call(conv_body, out_shape=(jax.ShapeDtypeStruct((2, 64, 64), F3...]
    reshape x1 -> x0, local copies, waits for them, and re-layouts: 1.85 us -> none  [shards(): return (velocity.reshape(2, 64, 64), decoded.reshape(2, 64, 2, 512))]
    unnamed x4 -> x2, local copies, waits for them, and re-layouts: 3.63 us -> 1.88 us
    pallas_call x1, Pallas kernels: 98.4 us -> 97.2 us  [shards(): pl.pallas_call(body, out_shape=(jax.ShapeDtypeStruct((ROWS, 64), F32), ja...]
where the time goes in v2:
time: 104 us
  Pallas kernels  99.7 us (96%)
  local copies, waits for them, and re-layouts  3.03 us (3%)
  between operations  1.31 us (1%)
    pallas_call x1, Pallas kernels, shards(): pl.pallas_call(body, out_shape=(jax.ShapeDtypeStruct((ROWS, 64), F32), ja...  97.2 us
    pallas_call x1, Pallas kernels, shards(): pl.pallas_call(conv_body, out_shape=(jax.ShapeDtypeStruct((2, 64, 64), F3...  2.43 us

profile of v2, /device:TPU:3, one launch (start us, length us, event | category | flops | bytes accessed | tf_op | source)
XLA Modules:
  0.0 104.0 jit_solution(4252948161094038711)
XLA Ops:
  0.6 0.0 copy-start
  0.6 1.9 %copy-done = bf16[1,256,2,24,128]{4,3,2,1,0:T(8,128)(2,1)S(1)} copy-done((bf16[1,256,2,24,128]{4,3,2,1,0:T(8,128)(2,1)S(1)}, bf16[1,256,2,24,128]{4,3,2,1,0:T(8,128)(2,1)}, u32[]{:S(2)}) %copy-start) | copy-done | bytes 3145752
  2.5 0.3 constant_dynamic-slice_fusion
  2.9 0.8 copy.16
  4.3 97.2 %shard_map.131 = (f32[128,64]{1,0:T(8,128)}, bf16[2,128,64]{2,1,0:T(8,128)(2,1)}) custom-call(bf16[1,2,64,9216]{3,2,1,0:T(8,128)(2,1)} %qkv.1, bf16[1,2,64,3072]{3,2,1,0:T(8,128)(2,1)} %residual.1, bf16[3,2,256,128]{3,2,1,0:T(8,128)(2,1)} %bitcast.9, s32[1]{0:T(128)S(6)} %copy.17.tlen, s32[1,256]{1,0:T(1,128)} %keep.1, f32[1,3072]{1,0:T(1,128)} %gate.1, ...), custom_call_target="tpu_custom_call" | custom-call | tf_op jit(solution)/shard_map/pallas_call | solution.py:400
  101.6 2.4 %shard_map.132 = (f32[2,64,64]{2,1,0:T(8,128)}, bf16[2,64,2,512]{3,2,1,0:T(2,128)(2,1)}) custom-call(f32[128,64]{1,0:T(8,128)} %get-tuple-element.4.guided, bf16[2,128,64]{2,1,0:T(8,128)(2,1)} %get-tuple-element.5.latents, bf16[48,512]{1,0:T(8,128)(2,1)} %bitcast.12, f32[1,512]{1,0:T(1,128)} %bitcast.13), custom_call_target="tpu_custom_call" | custom-call | tf_op jit(solution)/shard_map/pallas_call | solution.py:466
Async XLA Ops:
  0.6 1.9 %copy-start = (bf16[1,256,2,24,128]{4,3,2,1,0:T(8,128)(2,1)S(1)}, bf16[1,256,2,24,128]{4,3,2,1,0:T(8,128)(2,1)}, u32[]{:S(2)}) copy-start(bf16[1,256,2,24,128]{4,3,2,1,0:T(8,128)(2,1)} %param.14) | copy-start | bytes 9437188

commit v3 on v2

--- a/solution.py
+++ b/solution.py
@@ -109,12 +109,14 @@
             def _():
                 pltpu.make_async_copy(piece(s), landing, rcvs[kind].at[h]).start()
 
-    def share_head(h):
+    def share_keys(h):
         for kind in range(2):
             wait_bytes(kv.at[h, 0, c, kind], (rcv_k, rcv_v)[kind].at[h])
             mine = kv.at[h, 0, c, kind]
             remote(mine, kv.at[h, 1, c, kind], ysnd.at[h, kind], yrcv.at[h, kind], to_k).start()
             remote(mine, mine, dsnd.at[h, 0, kind], drcv.at[h, 0, kind], to_core).start()
+
+    def share_queries(h):
         wait_bytes(qb.at[h, 0], rcv_q.at[h])
         remote(qb.at[h, 0], qb.at[h, 1], ysnd.at[h, 2], yrcv.at[h, 2], to_q).start()
 
@@ -144,11 +146,6 @@
     fetch_r.start()
     fetch_f.start()
 
-    text_own.wait()
-    mask_own.wait()
-    wait_bytes(tb.at[1 - c], trcv.at[0])
-    wait_bytes(mb.at[1 - c], trcv.at[1])
-
     def queries(h, r, u):
         return qb[h, r, pl.ds(2 * u, 2)].reshape(QB, HD)
 
@@ -161,33 +158,37 @@
 
     blocks = 1024 // QB
 
-    def text_step(h):
-        keys = tb[xl, h, 0]
-        values = tb[xl, h, 1]
-        added = mb[xl]
-        par = h % 2
-        for u in range(blocks):
-            rows = pl.ds(u * QB, QB)
-            sc = scores(queries(h, 0, u), keys) + added[0:1]
-            top = jnp.max(sc, axis=1, keepdims=True)
-            out = weigh(jnp.exp2((sc - top) * SCALE), values)
-            m_s[par, 0, rows] = jnp.broadcast_to(top, (QB, HD))
-            acc[par, 0, rows] = out[:, :HD]
-            l_s[par, 0, rows] = out[:, HD:]
-
-    def softmax_blocks(h, far, rowsets, done):
+    def softmax_blocks(h, far, rowsets, done=None):
         keys = kv[h, far, :, 0].reshape(2048, HD)
         values = kv[h, far, :, 1].reshape(2048, HD)
+        with_text = far == 0 and rowsets == (0,)
+        if with_text:
+            text_keys = tb[xl, h, 0]
+            text_values = tb[xl, h, 1]
+            added = mb[xl]
         par = h % 2
         order = [(r, u) for r in rowsets for u in range(blocks)]
-        now = scores(queries(h, *order[0]), keys)
+
+        def all_scores(r, u):
+            q = queries(h, r, u)
+            if not with_text:
+                return scores(q, keys), None
+            return scores(q, keys), scores(q, text_keys) + added[0:1]
+
+        ahead = all_scores(*order[0])
         for i, (r, u) in enumerate(order):
-            later = scores(queries(h, *order[i + 1]), keys) if i + 1 < len(order) else None
+            now, now_text = ahead
+            if i + 1 < len(order):
+                ahead = all_scores(*order[i + 1])
             rows = pl.ds(u * QB, QB)
             top = jnp.max(now, axis=1, keepdims=True)
-            if far == 0 and r == 1:
+            if far == 0:
+                if with_text:
+                    top = jnp.maximum(top, jnp.max(now_text, axis=1, keepdims=True))
                 new = jnp.broadcast_to(top, (QB, HD))
                 out = weigh(jnp.exp2((now - top) * SCALE), values)
+                if with_text:
+                    out = out + weigh(jnp.exp2((now_text - top) * SCALE), text_values)
                 total, weight = out[:, :HD], out[:, HD:]
             else:
                 old = m_s[par, r, rows]
@@ -202,7 +203,6 @@
                 m_s[par, r, rows] = new
                 acc[par, r, rows] = total
                 l_s[par, r, rows] = weight
-            now = later
 
     def far_step(h):
         def done(u, top, total, weight):
@@ -263,42 +263,52 @@
 
         lax.fori_loop(0, D // 512, columns, 0)
 
+    def own_step(h):
+        wait_core(h, 0)
+        softmax_blocks(h, 0, (0,))
+
+    def shared_step(h):
+        wait_bytes(qb.at[h, 1], yrcv.at[h, 2])
+        softmax_blocks(h, 0, (1,))
+
+    share_keys(0)
+    share_queries(0)
     proj[...] = jnp.zeros_like(proj)
-    share_head(0)
-    wait_core(0, 0)
-    text_step(0)
-    softmax_blocks(0, 0, (0,), None)
-    wait_bytes(qb.at[0, 1], yrcv.at[0, 2])
-    softmax_blocks(0, 0, (1,), None)
+    text_own.wait()
+    mask_own.wait()
+    wait_bytes(tb.at[1 - c], trcv.at[0])
+    wait_bytes(mb.at[1 - c], trcv.at[1])
+    own_step(0)
+    share_keys(1)
+    pass_far(0)
+    shared_step(0)
 
     def step(h, carry):
         @pl.when(h < 2)
         def _():
-            share_head(h + 1)
-
-        pass_far(h)
+            share_queries(h + 1)
+            own_step(h + 1)
+
+        @pl.when(h == 2)
+        def _():
+            fetch_w.wait()
+            project(0)
+
+        wait_core(h, 1)
+        far_step(h)
+
+        @pl.when(h == 0)
+        def _():
+            share_keys(2)
 
         @pl.when(h < 2)
         def _():
-            wait_core(h + 1, 0)
-            text_step(h + 1)
-            softmax_blocks(h + 1, 0, (0,), None)
-
-        @pl.when(h == 1)
+            pass_far(h + 1)
+            shared_step(h + 1)
+
+        @pl.when(h == 2)
         def _():
-            fetch_w.wait()
-
-        @pl.when(h > 0)
-        def _():
-            project(h - 1)
-
-        wait_core(h, 1)
-        far_step(h)
-
-        @pl.when(h < 2)
-        def _():
-            wait_bytes(qb.at[h + 1, 1], yrcv.at[h + 1, 2])
-            softmax_blocks(h + 1, 0, (1,), None)
+            project(1)
 
         join(h)
         return carry

time: 104 us -> 94 us (0.904)
  Pallas kernels: 99.7 us -> 89.4 us
    pallas_call x1, Pallas kernels: 97.2 us -> 87 us  [shards(): pl.pallas_call(body, out_shape=(jax.ShapeDtypeStruct((ROWS, 64), F32), ja...]
where the time goes in v3:
time: 94 us; the launch traced here: 93.7 us
  Pallas kernels  89.4 us (95%)
  local copies, waits for them, and re-layouts  3.03 us (3%)
  between operations  1.31 us (1%)
    pallas_call x1, Pallas kernels, shards(): pl.pallas_call(body, out_shape=(jax.ShapeDtypeStruct((ROWS, 64), F32), ja...  87 us
    pallas_call x1, Pallas kernels, shards(): pl.pallas_call(conv_body, out_shape=(jax.ShapeDtypeStruct((2, 64, 64), F3...  2.44 us
    unnamed x2, local copies, waits for them, and re-layouts  1.88 us

profile of v3, /device:TPU:3, one launch (start us, length us, event | category | flops | bytes accessed | tf_op | source)
XLA Modules:
  0.0 93.7 jit_solution(13107211381402693372)
XLA Ops:
  0.6 0.0 copy-start
  0.6 1.9 %copy-done = bf16[1,256,2,24,128]{4,3,2,1,0:T(8,128)(2,1)S(1)} copy-done((bf16[1,256,2,24,128]{4,3,2,1,0:T(8,128)(2,1)S(1)}, bf16[1,256,2,24,128]{4,3,2,1,0:T(8,128)(2,1)}, u32[]{:S(2)}) %copy-start) | copy-done | bytes 3145752
  2.5 0.3 constant_dynamic-slice_fusion
  2.9 0.8 copy.16
  4.3 87.0 %shard_map.131 = (f32[128,64]{1,0:T(8,128)}, bf16[2,128,64]{2,1,0:T(8,128)(2,1)}) custom-call(bf16[1,2,64,9216]{3,2,1,0:T(8,128)(2,1)} %qkv.1, bf16[1,2,64,3072]{3,2,1,0:T(8,128)(2,1)} %residual.1, bf16[3,2,256,128]{3,2,1,0:T(8,128)(2,1)} %bitcast.9, s32[1]{0:T(128)S(6)} %copy.17.tlen, s32[1,256]{1,0:T(1,128)} %keep.1, f32[1,3072]{1,0:T(1,128)} %gate.1, ...), custom_call_target="tpu_custom_call" | custom-call | tf_op jit(solution)/shard_map/pallas_call | solution.py:410
  91.3 2.4 %shard_map.132 = (f32[2,64,64]{2,1,0:T(8,128)}, bf16[2,64,2,512]{3,2,1,0:T(2,128)(2,1)}) custom-call(f32[128,64]{1,0:T(8,128)} %get-tuple-element.4.guided, bf16[2,128,64]{2,1,0:T(8,128)(2,1)} %get-tuple-element.5.latents, bf16[48,512]{1,0:T(8,128)(2,1)} %bitcast.12, f32[1,512]{1,0:T(1,128)} %bitcast.13), custom_call_target="tpu_custom_call" | custom-call | tf_op jit(solution)/shard_map/pallas_call | solution.py:476
Async XLA Ops:
  0.6 1.9 %copy-start = (bf16[1,256,2,24,128]{4,3,2,1,0:T(8,128)(2,1)S(1)}, bf16[1,256,2,24,128]{4,3,2,1,0:T(8,128)(2,1)}, u32[]{:S(2)}) copy-start(bf16[1,256,2,24,128]{4,3,2,1,0:T(8,128)(2,1)} %param.14) | copy-start | bytes 9437188

commit v4 on v3

--- a/solution.py
+++ b/solution.py
@@ -31,10 +31,10 @@
 
 
 def body(
-    qkv, residual, text, tlen, keep, gate, w_out, fmod, w_fin, noisy,
+    qkv, residual, text_kv, tlen, keep, gate, w_out, fmod, w_fin, noisy,
     guided_out, latents,
-    qb, kv, ob, att, po, pr, so, sr, tb, mo, mb, wo, res, wf, proj, mod, pb, lat, halo, acc, m_s, l_s,
-    snd, rcv_q, rcv_k, rcv_v, ysnd, yrcv, dsnd, drcv, psnd, prcv, osnd, orcv, lsem, tsnd, trcv, gsnd, grcv, hsnd, hrcv,
+    qb, kv, ob, att, po, pr, so, sr, ta, tb, mo, mb, wo, res, wf, proj, mod, pb, lat, halo, acc, m_s, l_s,
+    snd, rcv_q, rcv_k, rcv_v, ysnd, yrcv, qsnd, qrcv, dsnd, drcv, psnd, prcv, osnd, orcv, lsem, tsnd, trcv, xsnd, xrcv, gsnd, grcv, hsnd, hrcv,
 ):
     c = lax.axis_index("cfg")
     b = lax.axis_index("blk")
@@ -109,45 +109,83 @@
             def _():
                 pltpu.make_async_copy(piece(s), landing, rcvs[kind].at[h]).start()
 
-    def share_keys(h):
+    def share_half(h, half, kind):
+        part = pl.ds(4 * half, 4)
+        mine = kv.at[h, 0, c, kind, part]
+        remote(mine, kv.at[h, 1, c, kind, part], ysnd.at[h, half, kind], yrcv.at[h, half, kind], to_k).start()
+
+    def share_keys(h, by_half=False):
         for kind in range(2):
-            wait_bytes(kv.at[h, 0, c, kind], (rcv_k, rcv_v)[kind].at[h])
             mine = kv.at[h, 0, c, kind]
-            remote(mine, kv.at[h, 1, c, kind], ysnd.at[h, kind], yrcv.at[h, kind], to_k).start()
+            wait_bytes(mine, (rcv_k, rcv_v)[kind].at[h])
+            if not by_half:
+                share_half(h, 0, kind)
+                share_half(h, 1, kind)
             remote(mine, mine, dsnd.at[h, 0, kind], drcv.at[h, 0, kind], to_core).start()
+        if by_half:
+            for half in range(2):
+                for kind in range(2):
+                    share_half(h, half, kind)
 
     def share_queries(h):
         wait_bytes(qb.at[h, 0], rcv_q.at[h])
-        remote(qb.at[h, 0], qb.at[h, 1], ysnd.at[h, 2], yrcv.at[h, 2], to_q).start()
-
-    def pass_far(h):
+        remote(qb.at[h, 0], qb.at[h, 1], qsnd.at[h], qrcv.at[h], to_q).start()
+
+    def pass_far(h, half):
         for kind in range(2):
-            far = kv.at[h, 1, c, kind]
-            wait_bytes(far, yrcv.at[h, kind])
-            remote(far, far, dsnd.at[h, 1, kind], drcv.at[h, 1, kind], to_core).start()
-
-    def wait_core(h, far):
+            far = kv.at[h, 1, c, kind, pl.ds(4 * half, 4)]
+            wait_bytes(far, yrcv.at[h, half, kind])
+            remote(far, far, dsnd.at[h, 1 + half, kind], drcv.at[h, 1 + half, kind], to_core).start()
+
+    def wait_own(h):
         for kind in range(2):
-            wait_bytes(kv.at[h, far, 1 - c, kind], drcv.at[h, far, kind])
-
-    text_own = pltpu.make_async_copy(text, tb.at[c], lsem.at[3])
-    text_out = remote(text, tb.at[c], tsnd.at[0], trcv.at[0], to_core)
+            wait_bytes(kv.at[h, 0, 1 - c, kind], drcv.at[h, 0, kind])
+
+    def wait_far(h, half):
+        for kind in range(2):
+            wait_bytes(kv.at[h, 1, 1 - c, kind, pl.ds(4 * half, 4)], drcv.at[h, 1 + half, kind])
+
+    fetch_t = pltpu.make_async_copy(text_kv.at[0], ta, lsem.at[3])
     mask_own = pltpu.make_async_copy(mo, mb.at[c], lsem.at[4])
     mask_out = remote(mo, mb.at[c], tsnd.at[1], trcv.at[1], to_core)
 
+    def take_text(kind):
+        def some(n, carry):
+            tokens = pl.ds(pl.multiple_of(n * 32, 32), 32)
+            found = ta[tokens, kind].astype(F32)
+            head = lax.broadcasted_iota(jnp.int32, (32, H, HD), 1)
+            for g in range(G):
+                row = jnp.sum(jnp.where(head == s * G + g, found, 0.0), axis=1)
+                tb[c, kind, g, tokens] = row.astype(BF)
+            return carry
+
+        lax.fori_loop(0, TXT // 32, some, 0)
+        remote(tb.at[c, kind], tb.at[c, kind], xsnd.at[kind], xrcv.at[kind], to_core).start()
+
+    fetch_t.start()
     send_head(0)
-    text_own.start()
-    text_out.start()
     mask_own.start()
     mask_out.start()
     send_head(1)
+    fetch_t.wait()
+    take_text(0)
+    share_keys(0)
     send_head(2)
+    take_text(1)
     fetch_w.start()
     fetch_r.start()
     fetch_f.start()
 
+    blocks = 1024 // QB
+
+    def place(u):
+        return (u + s // 2) % blocks
+
+    def rows_of(u):
+        return pl.ds(pl.multiple_of(place(u) * QB, QB), QB)
+
     def queries(h, r, u):
-        return qb[h, r, pl.ds(2 * u, 2)].reshape(QB, HD)
+        return qb[h, r, pl.ds(2 * place(u), 2)].reshape(QB, HD)
 
     def scores(q, keys):
         return lax.dot_general(q, keys, (((1,), (1,)), ((), ())), preferred_element_type=F32)
@@ -156,15 +194,14 @@
         padded = jnp.concatenate([values, jnp.ones_like(values)], axis=1)
         return jnp.dot(weights.astype(BF), padded, preferred_element_type=F32)
 
-    blocks = 1024 // QB
-
-    def softmax_blocks(h, far, rowsets, done=None):
-        keys = kv[h, far, :, 0].reshape(2048, HD)
-        values = kv[h, far, :, 1].reshape(2048, HD)
+    def softmax_blocks(h, far, rowsets, done=None, half=None):
+        part = slice(0, 8) if half is None else slice(4 * half, 4 * half + 4)
+        keys = kv[h, far, :, 0, part].reshape(-1, HD)
+        values = kv[h, far, :, 1, part].reshape(-1, HD)
         with_text = far == 0 and rowsets == (0,)
         if with_text:
-            text_keys = tb[xl, h, 0]
-            text_values = tb[xl, h, 1]
+            text_keys = tb[xl, 0, h]
+            text_values = tb[xl, 1, h]
             added = mb[xl]
         par = h % 2
         order = [(r, u) for r in rowsets for u in range(blocks)]
@@ -180,7 +217,7 @@
             now, now_text = ahead
             if i + 1 < len(order):
                 ahead = all_scores(*order[i + 1])
-            rows = pl.ds(u * QB, QB)
+            rows = rows_of(u)
             top = jnp.max(now, axis=1, keepdims=True)
             if far == 0:
                 if with_text:
@@ -197,34 +234,35 @@
                 out = weigh(jnp.exp2((now - new[:, :1]) * SCALE), values)
                 total = acc[par, r, rows] * factor + out[:, :HD]
                 weight = l_s[par, r, rows] * factor + out[:, HD:]
-            if r == 1 and far == 1:
+            if r == 1 and far == 1 and done is not None:
                 done(u, new, total, weight)
             else:
                 m_s[par, r, rows] = new
                 acc[par, r, rows] = total
                 l_s[par, r, rows] = weight
 
-    def far_step(h):
-        def done(u, top, total, weight):
-            cols = pl.ds(u * QB, QB)
+    def send_partial(h):
+        def done(i, top, total, weight):
+            u = place(i)
+            cols = rows_of(i)
             po[h, pl.ds(2 * u, 2)] = (total / weight).astype(BF).reshape(2, 2, 64, HD)
             lane = lax.broadcasted_iota(jnp.int32, (QB, HD), 1)
-            so[h, :, cols] = jnp.where(lane == 0, top, weight).T[0:8]
+            so[h, u] = jnp.where(lane == 0, top, weight).T[0:8]
             part = po.at[h, pl.ds(2 * u, 2)]
-            remote(part, pr.at[h, pl.ds(2 * u, 2)], psnd.at[h, 0], prcv.at[h, 0], to_q).start()
-            remote(so.at[h, :, cols], sr.at[h, :, cols], psnd.at[h, 1], prcv.at[h, 1], to_q).start()
-
-        softmax_blocks(h, 1, (1, 0), done)
+            remote(part, pr.at[h, pl.ds(2 * u, 2)], psnd.at[h, 0, u], prcv.at[h, 0, u], to_q).start()
+            remote(so.at[h, u], sr.at[h, u], psnd.at[h, 1, u], prcv.at[h, 1, u], to_q).start()
+
+        return done
 
     def join(h):
-        wait_bytes(pr.at[h], prcv.at[h, 0])
-        wait_bytes(sr.at[h], prcv.at[h, 1])
         par = h % 2
 
         def block(j, carry):
-            u = (j + s // 2) % blocks
-            rows = pl.ds(pl.multiple_of(u * QB, QB), QB)
-            stats = sr[h, :, rows].T
+            u = place(j)
+            rows = rows_of(j)
+            wait_bytes(pr.at[h, pl.ds(2 * u, 2)], prcv.at[h, 0, u])
+            wait_bytes(sr.at[h, u], prcv.at[h, 1, u])
+            stats = sr[h, u].T
             top_p = stats[:, 0:1]
             sum_p = stats[:, 1:2]
             top_a = m_s[par, 0, rows]
@@ -264,56 +302,87 @@
         lax.fori_loop(0, D // 512, columns, 0)
 
     def own_step(h):
-        wait_core(h, 0)
+        wait_own(h)
         softmax_blocks(h, 0, (0,))
 
     def shared_step(h):
-        wait_bytes(qb.at[h, 1], yrcv.at[h, 2])
+        wait_bytes(qb.at[h, 1], qrcv.at[h])
         softmax_blocks(h, 0, (1,))
 
-    share_keys(0)
+    proj[...] = jnp.zeros_like(proj)
+    mask_own.wait()
     share_queries(0)
-    proj[...] = jnp.zeros_like(proj)
-    text_own.wait()
-    mask_own.wait()
-    wait_bytes(tb.at[1 - c], trcv.at[0])
+    for kind in range(2):
+        wait_bytes(tb.at[1 - c, kind], xrcv.at[kind])
     wait_bytes(mb.at[1 - c], trcv.at[1])
     own_step(0)
     share_keys(1)
-    pass_far(0)
+    pass_far(0, 0)
+    pass_far(0, 1)
     shared_step(0)
 
     def step(h, carry):
-        @pl.when(h < 2)
-        def _():
-            share_queries(h + 1)
-            own_step(h + 1)
-
-        @pl.when(h == 2)
-        def _():
-            fetch_w.wait()
-            project(0)
-
-        wait_core(h, 1)
-        far_step(h)
+        share_queries(h + 1)
+        own_step(h + 1)
+        wait_far(h, 0)
+        wait_far(h, 1)
+        softmax_blocks(h, 1, (1, 0), send_partial(h))
 
         @pl.when(h == 0)
         def _():
-            share_keys(2)
-
-        @pl.when(h < 2)
+            share_keys(2, True)
+            pass_far(1, 0)
+            pass_far(1, 1)
+
+        @pl.when(h == 1)
         def _():
-            pass_far(h + 1)
-            shared_step(h + 1)
-
-        @pl.when(h == 2)
-        def _():
-            project(1)
-
+            pass_far(2, 0)
+
+        shared_step(h + 1)
         join(h)
         return carry
 
-    lax.fori_loop(0, G, step, 0)
+    lax.fori_loop(0, 2, step, 0)
+    pass_far(2, 1)
+    fetch_w.wait()
+    project(0)
+    wait_far(2, 0)
+    softmax_blocks(2, 1, (1,), None, 0)
+    wait_far(2, 1)
+    softmax_blocks(2, 1, (1,), send_partial(2), 1)
+    softmax_blocks(2, 1, (0,))
+    project(1)
+    join(2)
+
+    def wait_out(h):
+        wait_bytes(ob.at[h, pl.ds(0, 7)], osnd.at[h])
+
+        @pl.when(moved)
+        def _():
+            wait_bytes(ob.at[h, 0], osnd.at[h])
+
+    for h in range(G):
+        for kind in range(3):
+            wait_bytes(qb.at[h, 0, pl.ds(0, 7)], snd.at[h, kind])
+
+            @pl.when(moved)
+            def _():
+                wait_bytes(qb.at[h, 0, 0], snd.at[h, kind])
+
+        wait_bytes(qb.at[h, 0], qsnd.at[h])
+        for kind in range(2):
+            wait_bytes(kv.at[h, 0, c, 0], dsnd.at[h, 0, kind])
+            for half in range(2):
+                wait_bytes(kv.at[h, 0, c, 0, pl.ds(0, 4)], ysnd.at[h, half, kind])
+                wait_bytes(kv.at[h, 0, c, 0, pl.ds(0, 4)], dsnd.at[h, 1 + half, kind])
+        for u in range(blocks):
+            wait_bytes(po.at[h, pl.ds(0, 2)], psnd.at[h, 0, u])
+            wait_bytes(so.at[h, 0], psnd.at[h, 1, u])
+    for kind in range(2):
+        wait_bytes(tb.at[c, kind], xsnd.at[kind])
+    wait_bytes(mb.at[c], tsnd.at[1])
+    wait_out(0)
+    wait_out(1)
     project(G - 1)
 
     fetch_r.wait()
@@ -352,28 +421,7 @@
         wait_bytes(halo, hrcv)
         latents[0] = halo[...]
 
-    for h in range(G):
-        for kind in range(3):
-            wait_bytes(qb.at[h, 0, pl.ds(0, 7)], snd.at[h, kind])
-
-            @pl.when(moved)
-            def _():
-                wait_bytes(qb.at[h, 0, 0], snd.at[h, kind])
-
-            wait_bytes(kv.at[h, 0, c, 0], ysnd.at[h, kind])
-        for far in range(2):
-            for kind in range(2):
-                wait_bytes(kv.at[h, 0, c, 0], dsnd.at[h, far, kind])
-        wait_bytes(po.at[h], psnd.at[h, 0])
-        wait_bytes(so.at[h], psnd.at[h, 1])
-        wait_bytes(ob.at[h, pl.ds(0, 7)], osnd.at[h])
-
-        @pl.when(moved)
-        def _():
-            wait_bytes(ob.at[h, 0], osnd.at[h])
-
-    wait_bytes(tb.at[c], tsnd.at[0])
-    wait_bytes(mb.at[c], tsnd.at[1])
+    wait_out(2)
     wait_bytes(pb.at[c], gsnd)
 
     @pl.when(b < 7)
@@ -401,8 +449,6 @@
 
 
 def shards(qkv, residual, text_kv, text_len, text_keep, attn_gate, w_out, final_mod, w_final, noisy, conv_weight, conv_bias):
-    text = lax.dynamic_slice_in_dim(text_kv[0], lax.axis_index("sp") * G, G, axis=2)
-    text = jnp.transpose(text, (2, 1, 0, 3))
     hbm = pl.BlockSpec(memory_space=pl.ANY)
     vmem = pl.BlockSpec(memory_space=pltpu.VMEM)
     smem = pl.BlockSpec(memory_space=pltpu.SMEM)
@@ -413,7 +459,7 @@
             jax.ShapeDtypeStruct((ROWS, 64), F32),
             jax.ShapeDtypeStruct((2, ROWS, 64), BF),
         ),
-        in_specs=[hbm, hbm, vmem, smem, vmem, vmem, hbm, vmem, hbm, vmem],
+        in_specs=[hbm, hbm, hbm, smem, vmem, vmem, hbm, vmem, hbm, vmem],
         out_specs=(vmem, vmem),
         scratch_shapes=[
             pltpu.VMEM((G, 2, 8, 2, 64, HD), BF),
@@ -422,9 +468,10 @@
             pltpu.VMEM((8, G, 2, 64, HD), BF),
             pltpu.VMEM((G, 8, 2, 64, HD), BF),
             pltpu.VMEM((G, 8, 2, 64, HD), BF),
-            pltpu.VMEM((G, 8, 1024), F32),
-            pltpu.VMEM((G, 8, 1024), F32),
-            pltpu.VMEM((2, G, 2, TXT, HD), BF),
+            pltpu.VMEM((G, 4, 8, QB), F32),
+            pltpu.VMEM((G, 4, 8, QB), F32),
+            pltpu.VMEM((TXT, 2, H, HD), BF),
+            pltpu.VMEM((2, 2, G, TXT, HD), BF),
             pltpu.VMEM((8, TXT), F32),
             pltpu.VMEM((2, 8, TXT), F32),
             pltpu.VMEM((D, D), BF),
@@ -442,15 +489,19 @@
             dma((G,)),
             dma((G,)),
             dma((G,)),
-            dma((G, 3)),
-            dma((G, 3)),
             dma((G, 2, 2)),
             dma((G, 2, 2)),
-            dma((G, 2)),
-            dma((G, 2)),
+            dma((G,)),
+            dma((G,)),
+            dma((G, 3, 2)),
+            dma((G, 3, 2)),
+            dma((G, 2, 4)),
+            dma((G, 2, 4)),
             dma((G,)),
             dma((G,)),
             dma((5,)),
+            dma((2,)),
+            dma((2,)),
             dma((2,)),
             dma((2,)),
             dma,
@@ -464,7 +515,7 @@
     )(
         qkv,
         residual,
-        text,
+        text_kv,
         text_len,
         text_keep,
         attn_gate,

time: 94 us -> 92.2 us (0.981)
  local copies, waits for them, and re-layouts: 3.03 us -> 0 us
  Pallas kernels: 89.4 us -> 90.7 us
    unnamed x2 -> x0, local copies, waits for them, and re-layouts: 1.88 us -> none
    pallas_call x1, Pallas kernels: 87 us -> 88.2 us  [shards(): pl.pallas_call(body, out_shape=(jax.ShapeDtypeStruct((ROWS, 64), F32), ja...]
    dynamic_slice x2 -> x0, local copies, waits for them, and re-layouts: 1.15 us -> none  [shards(): lax.dynamic_slice_in_dim(text_kv[0], lax.axis_index('sp') * G, G, axis=2)]
where the time goes in v4:
time: 92.2 us; the launch traced here: 91.9 us
  Pallas kernels  90.7 us (98%)
  between operations  1.29 us (1%)
    pallas_call x1, Pallas kernels, shards(): pl.pallas_call(body, out_shape=(jax.ShapeDtypeStruct((ROWS, 64), F32), ja...  88.2 us
    pallas_call x1, Pallas kernels, shards(): pl.pallas_call(conv_body, out_shape=(jax.ShapeDtypeStruct((2, 64, 64), F3...  2.43 us

profile of v4, /device:TPU:3, one launch (start us, length us, event | category | flops | bytes accessed | tf_op | source)
XLA Modules:
  0.0 91.9 jit_solution(4914702163194344710)
XLA Ops:
  1.3 88.2 %shard_map.131 = (f32[128,64]{1,0:T(8,128)}, bf16[2,128,64]{2,1,0:T(8,128)(2,1)}) custom-call(bf16[1,2,64,9216]{3,2,1,0:T(8,128)(2,1)} %qkv.1, bf16[1,2,64,3072]{3,2,1,0:T(8,128)(2,1)} %residual.1, bf16[1,256,2,24,128]{4,3,2,1,0:T(8,128)(2,1)} %text_kv.1, s32[1]{0:T(128)S(6)} %copy.14.tlen, s32[1,256]{1,0:T(1,128)} %keep.1, f32[1,3072]{1,0:T(1,128)} %gate.1, ...), custom_call_target="tpu_custom_call" | custom-call | tf_op jit(solution)/shard_map/pallas_call | solution.py:456
  89.5 2.4 %shard_map.132 = (f32[2,64,64]{2,1,0:T(8,128)}, bf16[2,64,2,512]{3,2,1,0:T(2,128)(2,1)}) custom-call(f32[128,64]{1,0:T(8,128)} %get-tuple-element.4.guided, bf16[2,128,64]{2,1,0:T(8,128)(2,1)} %get-tuple-element.5.latents, bf16[48,512]{1,0:T(8,128)(2,1)} %bitcast.6, f32[1,512]{1,0:T(1,128)} %bitcast.7), custom_call_target="tpu_custom_call" | custom-call | tf_op jit(solution)/shard_map/pallas_call | solution.py:527

commit v5 on v4

--- a/solution.py
+++ b/solution.py
@@ -33,21 +33,25 @@
 def body(
     qkv, residual, text_kv, tlen, keep, gate, w_out, fmod, w_fin, noisy,
     guided_out, latents,
-    qb, kv, ob, att, po, pr, so, sr, ta, tb, mo, mb, wo, res, wf, proj, mod, pb, lat, halo, acc, m_s, l_s,
-    snd, rcv_q, rcv_k, rcv_v, ysnd, yrcv, qsnd, qrcv, dsnd, drcv, psnd, prcv, osnd, orcv, lsem, tsnd, trcv, xsnd, xrcv, gsnd, grcv, hsnd, hrcv,
+    qb, kv, ob, att, ta, tb, mo, mb, wo, res, wf, proj, mod, pb, lat, halo, acc, m_s, l_s,
+    snd, rcv_q, rcv_k, rcv_v, ysnd, yrcv, qsnd, qrcv, dsnd, drcv, osnd, orcv, lsem, tsnd, trcv, xsnd, xrcv, gsnd, grcv, hsnd, hrcv,
 ):
     c = lax.axis_index("cfg")
     b = lax.axis_index("blk")
     s = lax.axis_index("sp")
     xl = b // 4
     y = b % 4
-    to_q = (c, xl * 4 + y + 1 - 2 * (y % 2), s)
+    yq = y + 1 - 2 * (y % 2)
+    to_q = (c, xl * 4 + yq, s)
     to_k = (c, xl * 4 + 3 - y, s)
     to_core = (1 - c, b, s)
     moved = c != xl
 
     def peer(d):
         return (xl, c * 4 + y, d)
+
+    def owner(r, d):
+        return (xl, c * 4 + (yq if r else y), d)
 
     def remote(src, dst, send, recv, dev):
         return pltpu.make_async_remote_copy(src, dst, send, recv, device_id=dev, device_id_type=MESH)
@@ -66,6 +70,8 @@
     sig(to_core)
     for j in range(1, 8):
         sig(peer((s + j) % 8))
+    for j in range(8):
+        sig(owner(1, (s + j) % 8))
 
     @pl.when(moved)
     def _():
@@ -79,10 +85,10 @@
     def _():
         sig((c, b - 1, s))
 
-    kept = (lax.broadcasted_iota(jnp.int32, (1, TXT), 1) < tlen[0]) & (keep[...] == 1)
+    kept = (lax.broadcasted_iota(jnp.int32, (1, TXT), 1) < tlen[...]) & (keep[...] == 1)
     mo[...] = jnp.broadcast_to(jnp.where(kept, 0.0, -1e30).astype(F32), (8, TXT))
 
-    count = 10 + jnp.where(moved, 1, 0) + jnp.where(b < 7, 1, 0) + jnp.where(b > 0, 1, 0)
+    count = 18 + jnp.where(moved, 1, 0) + jnp.where(b < 7, 1, 0) + jnp.where(b > 0, 1, 0)
     pl.semaphore_wait(bar, count)
 
     rcvs = (rcv_q, rcv_k, rcv_v)
@@ -234,62 +240,70 @@
                 out = weigh(jnp.exp2((now - new[:, :1]) * SCALE), values)
                 total = acc[par, r, rows] * factor + out[:, :HD]
                 weight = l_s[par, r, rows] * factor + out[:, HD:]
-            if r == 1 and far == 1 and done is not None:
-                done(u, new, total, weight)
+            if done is not None:
+                done(r, u, new, total, weight)
             else:
                 m_s[par, r, rows] = new
                 acc[par, r, rows] = total
                 l_s[par, r, rows] = weight
 
-    def send_partial(h):
-        def done(i, top, total, weight):
-            u = place(i)
-            cols = rows_of(i)
-            po[h, pl.ds(2 * u, 2)] = (total / weight).astype(BF).reshape(2, 2, 64, HD)
+    def finish(h):
+        def done(r, i, top, total, weight):
+            out = (total / weight).astype(BF)
             lane = lax.broadcasted_iota(jnp.int32, (QB, HD), 1)
-            so[h, u] = jnp.where(lane == 0, top, weight).T[0:8]
-            part = po.at[h, pl.ds(2 * u, 2)]
-            remote(part, pr.at[h, pl.ds(2 * u, 2)], psnd.at[h, 0, u], prcv.at[h, 0, u], to_q).start()
-            remote(so.at[h, u], sr.at[h, u], psnd.at[h, 1, u], prcv.at[h, 1, u], to_q).start()
+            stats = jnp.zeros((QB, HD), F32)
+            for at, value, pieces in ((0, top, 3), (3, weight, 2)):
+                for k in range(pieces):
+                    piece = value.astype(BF).astype(F32)
+                    stats = jnp.where(lane == at + k, piece, stats)
+                    value = value - piece
+            below = stats.T[0:16].astype(BF)
+            for k in range(2):
+                d = 2 * place(i) + k
+                ob[r, h, d, 0:ROWS] = out[k * ROWS : (k + 1) * ROWS]
+                ob[r, h, d, ROWS : ROWS + 16] = below[:, k * ROWS : (k + 1) * ROWS]
 
         return done
 
-    def join(h):
-        par = h % 2
-
-        def block(j, carry):
-            u = place(j)
-            rows = rows_of(j)
-            wait_bytes(pr.at[h, pl.ds(2 * u, 2)], prcv.at[h, 0, u])
-            wait_bytes(sr.at[h, u], prcv.at[h, 1, u])
-            stats = sr[h, u].T
-            top_p = stats[:, 0:1]
-            sum_p = stats[:, 1:2]
-            top_a = m_s[par, 0, rows]
-            new = jnp.maximum(top_a, top_p)
-            f_a = jnp.exp2((top_a - new) * SCALE)
-            f_p = jnp.exp2((top_p - new) * SCALE) * sum_p
-            partial = pr[h, pl.ds(2 * u, 2)].reshape(QB, HD).astype(F32)
-            out = (acc[par, 0, rows] * f_a + partial * f_p) / (l_s[par, 0, rows] * f_a + f_p)
-            ob[h, pl.ds(2 * u, 2)] = out.astype(BF).reshape(2, 2, 64, HD)
-            for k in range(2):
-                d = 2 * u + k
-
-                @pl.when(jnp.logical_or(moved, d != s))
-                def _():
-                    remote(ob.at[h, d], att.at[s, h], osnd.at[h], orcv.at[h], peer(d)).start()
-
-                @pl.when(jnp.logical_not(jnp.logical_or(moved, d != s)))
-                def _():
-                    pltpu.make_async_copy(ob.at[h, d], att.at[s, h], orcv.at[h]).start()
+    def send_out(h, r):
+        def one(j, carry):
+            d = (2 * (s // 2) + j) % 8
+            slab = ob.at[r, h, d]
+            landing = att.at[r, s, h]
+            if r:
+                remote(slab, landing, osnd.at[h, 1], orcv.at[h, 1], owner(1, d)).start()
+                return carry
+
+            @pl.when(jnp.logical_or(moved, d != s))
+            def _():
+                remote(slab, landing, osnd.at[h, 0], orcv.at[h, 0], owner(0, d)).start()
+
+            @pl.when(jnp.logical_not(jnp.logical_or(moved, d != s)))
+            def _():
+                pltpu.make_async_copy(slab, landing, orcv.at[h, 0]).start()
 
             return carry
 
-        lax.fori_loop(0, blocks, block, 0)
+        lax.fori_loop(0, 8, one, 0)
 
     def project(h):
-        wait_bytes(att.at[:, h], orcv.at[h])
-        rows = jnp.concatenate([att[d, h].reshape(ROWS, HD) for d in range(8)], axis=1)
+        tops, sums = [], []
+        for r in range(2):
+            wait_bytes(att.at[r, :, h], orcv.at[h, r])
+            stats = att[r, :, h, ROWS : ROWS + 16].astype(F32)
+            tops.append(stats[:, 0] + stats[:, 1] + stats[:, 2])
+            sums.append(stats[:, 3] + stats[:, 4])
+        top = jnp.maximum(tops[0], tops[1])
+        parts = [jnp.exp2((tops[r] - top) * SCALE) * sums[r] for r in range(2)]
+        whole = parts[0] + parts[1]
+        shares = [(part / whole).T for part in parts]
+        rows = jnp.concatenate(
+            [
+                sum(att[r, d, h, 0:ROWS].astype(F32) * shares[r][:, d : d + 1] for r in range(2)).astype(BF)
+                for d in range(8)
+            ],
+            axis=1,
+        )
 
         def columns(n, carry):
             cols = pl.ds(pl.multiple_of(n * 512, 512), 512)
@@ -326,7 +340,9 @@
         own_step(h + 1)
         wait_far(h, 0)
         wait_far(h, 1)
-        softmax_blocks(h, 1, (1, 0), send_partial(h))
+        softmax_blocks(h, 1, (1, 0), finish(h))
+        send_out(h, 1)
+        send_out(h, 0)
 
         @pl.when(h == 0)
         def _():
@@ -339,7 +355,6 @@
             pass_far(2, 0)
 
         shared_step(h + 1)
-        join(h)
         return carry
 
     lax.fori_loop(0, 2, step, 0)
@@ -347,19 +362,21 @@
     fetch_w.wait()
     project(0)
     wait_far(2, 0)
-    softmax_blocks(2, 1, (1,), None, 0)
+    softmax_blocks(2, 1, (1, 0), None, 0)
     wait_far(2, 1)
-    softmax_blocks(2, 1, (1,), send_partial(2), 1)
-    softmax_blocks(2, 1, (0,))
+    softmax_blocks(2, 1, (1,), finish(2), 1)
+    send_out(2, 1)
+    softmax_blocks(2, 1, (0,), finish(2), 1)
+    send_out(2, 0)
     project(1)
-    join(2)
 
     def wait_out(h):
-        wait_bytes(ob.at[h, pl.ds(0, 7)], osnd.at[h])
+        wait_bytes(ob.at[1, h], osnd.at[h, 1])
+        wait_bytes(ob.at[0, h, pl.ds(0, 7)], osnd.at[h, 0])
 
         @pl.when(moved)
         def _():
-            wait_bytes(ob.at[h, 0], osnd.at[h])
+            wait_bytes(ob.at[0, h, 0], osnd.at[h, 0])
 
     for h in range(G):
         for kind in range(3):
@@ -375,9 +392,6 @@
             for half in range(2):
                 wait_bytes(kv.at[h, 0, c, 0, pl.ds(0, 4)], ysnd.at[h, half, kind])
                 wait_bytes(kv.at[h, 0, c, 0, pl.ds(0, 4)], dsnd.at[h, 1 + half, kind])
-        for u in range(blocks):
-            wait_bytes(po.at[h, pl.ds(0, 2)], psnd.at[h, 0, u])
-            wait_bytes(so.at[h, 0], psnd.at[h, 1, u])
     for kind in range(2):
         wait_bytes(tb.at[c, kind], xsnd.at[kind])
     wait_bytes(mb.at[c], tsnd.at[1])
@@ -451,7 +465,6 @@
 def shards(qkv, residual, text_kv, text_len, text_keep, attn_gate, w_out, final_mod, w_final, noisy, conv_weight, conv_bias):
     hbm = pl.BlockSpec(memory_space=pl.ANY)
     vmem = pl.BlockSpec(memory_space=pltpu.VMEM)
-    smem = pl.BlockSpec(memory_space=pltpu.SMEM)
     dma = pltpu.SemaphoreType.DMA
     guided, latents = pl.pallas_call(
         body,
@@ -459,17 +472,13 @@
             jax.ShapeDtypeStruct((ROWS, 64), F32),
             jax.ShapeDtypeStruct((2, ROWS, 64), BF),
         ),
-        in_specs=[hbm, hbm, hbm, smem, vmem, vmem, hbm, vmem, hbm, vmem],
+        in_specs=[hbm, hbm, hbm, vmem, vmem, vmem, hbm, vmem, hbm, vmem],
         out_specs=(vmem, vmem),
         scratch_shapes=[
             pltpu.VMEM((G, 2, 8, 2, 64, HD), BF),
             pltpu.VMEM((G, 2, 2, 2, 8, 2, 64, HD), BF),
-            pltpu.VMEM((G, 8, 2, 64, HD), BF),
-            pltpu.VMEM((8, G, 2, 64, HD), BF),
-            pltpu.VMEM((G, 8, 2, 64, HD), BF),
-            pltpu.VMEM((G, 8, 2, 64, HD), BF),
-            pltpu.VMEM((G, 4, 8, QB), F32),
-            pltpu.VMEM((G, 4, 8, QB), F32),
+            pltpu.VMEM((2, G, 8, ROWS + 16, HD), BF),
+            pltpu.VMEM((2, 8, G, ROWS + 16, HD), BF),
             pltpu.VMEM((TXT, 2, H, HD), BF),
             pltpu.VMEM((2, 2, G, TXT, HD), BF),
             pltpu.VMEM((8, TXT), F32),
@@ -495,10 +504,8 @@
             dma((G,)),
             dma((G, 3, 2)),
             dma((G, 3, 2)),
-            dma((G, 2, 4)),
-            dma((G, 2, 4)),
-            dma((G,)),
-            dma((G,)),
+            dma((G, 2)),
+            dma((G, 2)),
             dma((5,)),
             dma((2,)),
             dma((2,)),
@@ -516,7 +523,7 @@
         qkv,
         residual,
         text_kv,
-        text_len,
+        text_len.reshape(1, 1),
         text_keep,
         attn_gate,
         w_out,

time: 92.2 us -> 88.3 us (0.958)
  Pallas kernels: 90.7 us -> 86.8 us
    pallas_call x1, Pallas kernels: 88.2 us -> 84.3 us  [shards(): pl.pallas_call(body, out_shape=(jax.ShapeDtypeStruct((ROWS, 64), F32), ja...]
where the time goes in v5:
time: 88.3 us; the launch traced here: 88 us
  Pallas kernels  86.8 us (98%)
  between operations  1.29 us (1%)
    pallas_call x1, Pallas kernels, shards(): pl.pallas_call(body, out_shape=(jax.ShapeDtypeStruct((ROWS, 64), F32), ja...  84.3 us
    pallas_call x1, Pallas kernels, shards(): pl.pallas_call(conv_body, out_shape=(jax.ShapeDtypeStruct((2, 64, 64), F3...  2.44 us

profile of v5, /device:TPU:3, one launch (start us, length us, event | category | flops | bytes accessed | tf_op | source)
XLA Modules:
  0.0 88.0 jit_solution(5979024355314574204)
XLA Ops:
  1.3 84.3 %shard_map.131 = (f32[128,64]{1,0:T(8,128)}, bf16[2,128,64]{2,1,0:T(8,128)(2,1)}) custom-call(bf16[1,2,64,9216]{3,2,1,0:T(8,128)(2,1)} %qkv.1, bf16[1,2,64,3072]{3,2,1,0:T(8,128)(2,1)} %residual.1, bf16[1,256,2,24,128]{4,3,2,1,0:T(8,128)(2,1)} %text_kv.1, s32[1,1]{1,0:T(1,128)} %bitcast.5.tlen, s32[1,256]{1,0:T(1,128)} %keep.1, f32[1,3072]{1,0:T(1,128)} %gate.1, ...), custom_call_target="tpu_custom_call" | custom-call | tf_op jit(solution)/shard_map/pallas_call | solution.py:469
  85.6 2.4 %shard_map.132 = (f32[2,64,64]{2,1,0:T(8,128)}, bf16[2,64,2,512]{3,2,1,0:T(2,128)(2,1)}) custom-call(f32[128,64]{1,0:T(8,128)} %get-tuple-element.4.guided, bf16[2,128,64]{2,1,0:T(8,128)(2,1)} %get-tuple-element.5.latents, bf16[48,512]{1,0:T(8,128)(2,1)} %bitcast.8, f32[1,512]{1,0:T(1,128)} %bitcast.9), custom_call_target="tpu_custom_call" | custom-call | tf_op jit(solution)/shard_map/pallas_call | solution.py:534

commit v6 on v5

--- a/solution.py
+++ b/solution.py
@@ -85,7 +85,7 @@
     def _():
         sig((c, b - 1, s))
 
-    kept = (lax.broadcasted_iota(jnp.int32, (1, TXT), 1) < tlen[...]) & (keep[...] == 1)
+    kept = (lax.broadcasted_iota(jnp.int32, (1, TXT), 1) < tlen[...].reshape(1, 1)) & (keep[...] == 1)
     mo[...] = jnp.broadcast_to(jnp.where(kept, 0.0, -1e30).astype(F32), (8, TXT))
 
     count = 18 + jnp.where(moved, 1, 0) + jnp.where(b < 7, 1, 0) + jnp.where(b > 0, 1, 0)
@@ -94,7 +94,7 @@
     rcvs = (rcv_q, rcv_k, rcv_v)
 
     def send_head(h):
-        for kind in (1, 2, 0):
+        for kind in (1, 0, 2):
             landing = qb.at[h, 0, s] if kind == 0 else kv.at[h, 0, xl, kind - 1, s]
 
             def piece(d):
@@ -115,41 +115,30 @@
             def _():
                 pltpu.make_async_copy(piece(s), landing, rcvs[kind].at[h]).start()
 
-    def share_half(h, half, kind):
-        part = pl.ds(4 * half, 4)
-        mine = kv.at[h, 0, c, kind, part]
-        remote(mine, kv.at[h, 1, c, kind, part], ysnd.at[h, half, kind], yrcv.at[h, half, kind], to_k).start()
-
-    def share_keys(h, by_half=False):
-        for kind in range(2):
-            mine = kv.at[h, 0, c, kind]
-            wait_bytes(mine, (rcv_k, rcv_v)[kind].at[h])
-            if not by_half:
-                share_half(h, 0, kind)
-                share_half(h, 1, kind)
-            remote(mine, mine, dsnd.at[h, 0, kind], drcv.at[h, 0, kind], to_core).start()
-        if by_half:
-            for half in range(2):
-                for kind in range(2):
-                    share_half(h, half, kind)
+    def share_keys(h, kind):
+        mine = kv.at[h, 0, c, kind]
+        wait_bytes(mine, (rcv_k, rcv_v)[kind].at[h])
+        remote(mine, kv.at[h, 1, c, kind], ysnd.at[h, kind], yrcv.at[h, kind], to_k).start()
+        remote(mine, mine, dsnd.at[h, 0, kind], drcv.at[h, 0, kind], to_core).start()
 
     def share_queries(h):
         wait_bytes(qb.at[h, 0], rcv_q.at[h])
         remote(qb.at[h, 0], qb.at[h, 1], qsnd.at[h], qrcv.at[h], to_q).start()
 
-    def pass_far(h, half):
+    def share(h):
+        share_keys(h, 0)
+        share_queries(h)
+        share_keys(h, 1)
+
+    def pass_far(h):
         for kind in range(2):
-            far = kv.at[h, 1, c, kind, pl.ds(4 * half, 4)]
-            wait_bytes(far, yrcv.at[h, half, kind])
-            remote(far, far, dsnd.at[h, 1 + half, kind], drcv.at[h, 1 + half, kind], to_core).start()
-
-    def wait_own(h):
+            far = kv.at[h, 1, c, kind]
+            wait_bytes(far, yrcv.at[h, kind])
+            remote(far, far, dsnd.at[h, 1, kind], drcv.at[h, 1, kind], to_core).start()
+
+    def wait_core(h, far):
         for kind in range(2):
-            wait_bytes(kv.at[h, 0, 1 - c, kind], drcv.at[h, 0, kind])
-
-    def wait_far(h, half):
-        for kind in range(2):
-            wait_bytes(kv.at[h, 1, 1 - c, kind, pl.ds(4 * half, 4)], drcv.at[h, 1 + half, kind])
+            wait_bytes(kv.at[h, far, 1 - c, kind], drcv.at[h, far, kind])
 
     fetch_t = pltpu.make_async_copy(text_kv.at[0], ta, lsem.at[3])
     mask_own = pltpu.make_async_copy(mo, mb.at[c], lsem.at[4])
@@ -175,9 +164,11 @@
     send_head(1)
     fetch_t.wait()
     take_text(0)
-    share_keys(0)
+    share_keys(0, 0)
     send_head(2)
     take_text(1)
+    share_queries(0)
+    share_keys(0, 1)
     fetch_w.start()
     fetch_r.start()
     fetch_f.start()
@@ -200,29 +191,26 @@
         padded = jnp.concatenate([values, jnp.ones_like(values)], axis=1)
         return jnp.dot(weights.astype(BF), padded, preferred_element_type=F32)
 
-    def softmax_blocks(h, far, rowsets, done=None, half=None):
-        part = slice(0, 8) if half is None else slice(4 * half, 4 * half + 4)
-        keys = kv[h, far, :, 0, part].reshape(-1, HD)
-        values = kv[h, far, :, 1, part].reshape(-1, HD)
-        with_text = far == 0 and rowsets == (0,)
+    def softmax_blocks(h, far, r, done=None):
+        keys = kv[h, far, :, 0].reshape(-1, HD)
+        values = kv[h, far, :, 1].reshape(-1, HD)
+        with_text = far == 0 and r == 0
         if with_text:
             text_keys = tb[xl, 0, h]
             text_values = tb[xl, 1, h]
             added = mb[xl]
-        par = h % 2
-        order = [(r, u) for r in rowsets for u in range(blocks)]
-
-        def all_scores(r, u):
+
+        def all_scores(u):
             q = queries(h, r, u)
             if not with_text:
                 return scores(q, keys), None
             return scores(q, keys), scores(q, text_keys) + added[0:1]
 
-        ahead = all_scores(*order[0])
-        for i, (r, u) in enumerate(order):
+        ahead = all_scores(0)
+        for u in range(blocks):
             now, now_text = ahead
-            if i + 1 < len(order):
-                ahead = all_scores(*order[i + 1])
+            if u + 1 < blocks:
+                ahead = all_scores(u + 1)
             rows = rows_of(u)
             top = jnp.max(now, axis=1, keepdims=True)
             if far == 0:
@@ -234,30 +222,31 @@
                     out = out + weigh(jnp.exp2((now_text - top) * SCALE), text_values)
                 total, weight = out[:, :HD], out[:, HD:]
             else:
-                old = m_s[par, r, rows]
+                old = m_s[r, rows]
                 new = jnp.maximum(old, top)
                 factor = jnp.exp2((old - new) * SCALE)
                 out = weigh(jnp.exp2((now - new[:, :1]) * SCALE), values)
-                total = acc[par, r, rows] * factor + out[:, :HD]
-                weight = l_s[par, r, rows] * factor + out[:, HD:]
+                total = acc[r, rows] * factor + out[:, :HD]
+                weight = l_s[r, rows] * factor + out[:, HD:]
             if done is not None:
-                done(r, u, new, total, weight)
+                done(u, new, total, weight)
             else:
-                m_s[par, r, rows] = new
-                acc[par, r, rows] = total
-                l_s[par, r, rows] = weight
-
-    def finish(h):
-        def done(r, i, top, total, weight):
+                m_s[r, rows] = new
+                acc[r, rows] = total
+                l_s[r, rows] = weight
+
+    def finish(h, r):
+        def done(i, top, total, weight):
             out = (total / weight).astype(BF)
             lane = lax.broadcasted_iota(jnp.int32, (QB, HD), 1)
-            stats = jnp.zeros((QB, HD), F32)
-            for at, value, pieces in ((0, top, 3), (3, weight, 2)):
-                for k in range(pieces):
-                    piece = value.astype(BF).astype(F32)
-                    stats = jnp.where(lane == at + k, piece, stats)
-                    value = value - piece
-            below = stats.T[0:16].astype(BF)
+            stats = jnp.where(lane == 0, top, weight).T[0:8]
+            high = stats.astype(BF)
+            rest = stats - high.astype(F32)
+            middle = rest.astype(BF)
+            low = rest - middle.astype(F32)
+            line = lax.broadcasted_iota(jnp.int32, (8, QB), 0)
+            second = jnp.where(line == 2, low[0:1], middle.astype(F32))
+            below = jnp.concatenate([high.astype(F32), second], axis=0).astype(BF)
             for k in range(2):
                 d = 2 * place(i) + k
                 ob[r, h, d, 0:ROWS] = out[k * ROWS : (k + 1) * ROWS]
@@ -291,8 +280,8 @@
         for r in range(2):
             wait_bytes(att.at[r, :, h], orcv.at[h, r])
             stats = att[r, :, h, ROWS : ROWS + 16].astype(F32)
-            tops.append(stats[:, 0] + stats[:, 1] + stats[:, 2])
-            sums.append(stats[:, 3] + stats[:, 4])
+            tops.append(stats[:, 0] + stats[:, 8] + stats[:, 10])
+            sums.append(stats[:, 1] + stats[:, 9])
         top = jnp.maximum(tops[0], tops[1])
         parts = [jnp.exp2((tops[r] - top) * SCALE) * sums[r] for r in range(2)]
         whole = parts[0] + parts[1]
@@ -315,59 +304,42 @@
 
         lax.fori_loop(0, D // 512, columns, 0)
 
-    def own_step(h):
-        wait_own(h)
-        softmax_blocks(h, 0, (0,))
-
-    def shared_step(h):
-        wait_bytes(qb.at[h, 1], qrcv.at[h])
-        softmax_blocks(h, 0, (1,))
-
     proj[...] = jnp.zeros_like(proj)
     mask_own.wait()
-    share_queries(0)
     for kind in range(2):
         wait_bytes(tb.at[1 - c, kind], xrcv.at[kind])
     wait_bytes(mb.at[1 - c], trcv.at[1])
-    own_step(0)
-    share_keys(1)
-    pass_far(0, 0)
-    pass_far(0, 1)
-    shared_step(0)
 
     def step(h, carry):
-        share_queries(h + 1)
-        own_step(h + 1)
-        wait_far(h, 0)
-        wait_far(h, 1)
-        softmax_blocks(h, 1, (1, 0), finish(h))
-        send_out(h, 1)
-        send_out(h, 0)
+        wait_core(h, 0)
+        softmax_blocks(h, 0, 0)
+
+        @pl.when(h == 1)
+        def _():
+            share(2)
+
+        @pl.when(h > 0)
+        def _():
+            pass_far(h)
+
+        wait_bytes(qb.at[h, 1], qrcv.at[h])
+        softmax_blocks(h, 0, 1)
 
         @pl.when(h == 0)
         def _():
-            share_keys(2, True)
-            pass_far(1, 0)
-            pass_far(1, 1)
-
-        @pl.when(h == 1)
-        def _():
-            pass_far(2, 0)
-
-        shared_step(h + 1)
+            pass_far(0)
+            share(1)
+
+        wait_core(h, 1)
+        softmax_blocks(h, 1, 1, finish(h, 1))
+        send_out(h, 1)
+        softmax_blocks(h, 1, 0, finish(h, 0))
+        send_out(h, 0)
         return carry
 
-    lax.fori_loop(0, 2, step, 0)
-    pass_far(2, 1)
+    lax.fori_loop(0, G, step, 0)
     fetch_w.wait()
     project(0)
-    wait_far(2, 0)
-    softmax_blocks(2, 1, (1, 0), None, 0)
-    wait_far(2, 1)
-    softmax_blocks(2, 1, (1,), finish(2), 1)
-    send_out(2, 1)
-    softmax_blocks(2, 1, (0,), finish(2), 1)
-    send_out(2, 0)
     project(1)
 
     def wait_out(h):
@@ -388,10 +360,9 @@
 
         wait_bytes(qb.at[h, 0], qsnd.at[h])
         for kind in range(2):
-            wait_bytes(kv.at[h, 0, c, 0], dsnd.at[h, 0, kind])
-            for half in range(2):
-                wait_bytes(kv.at[h, 0, c, 0, pl.ds(0, 4)], ysnd.at[h, half, kind])
-                wait_bytes(kv.at[h, 0, c, 0, pl.ds(0, 4)], dsnd.at[h, 1 + half, kind])
+            wait_bytes(kv.at[h, 0, c, 0], ysnd.at[h, kind])
+            for far in range(2):
+                wait_bytes(kv.at[h, 0, c, 0], dsnd.at[h, far, kind])
     for kind in range(2):
         wait_bytes(tb.at[c, kind], xsnd.at[kind])
     wait_bytes(mb.at[c], tsnd.at[1])
@@ -491,19 +462,19 @@
             pltpu.VMEM((2, ROWS, 64), F32),
             pltpu.VMEM((ROWS, 64), BF),
             pltpu.VMEM((ROWS, 64), BF),
-            pltpu.VMEM((2, 2, 1024, HD), F32),
-            pltpu.VMEM((2, 2, 1024, HD), F32),
-            pltpu.VMEM((2, 2, 1024, HD), F32),
+            pltpu.VMEM((2, 1024, HD), F32),
+            pltpu.VMEM((2, 1024, HD), F32),
+            pltpu.VMEM((2, 1024, HD), F32),
             dma((G, 3)),
             dma((G,)),
             dma((G,)),
             dma((G,)),
+            dma((G, 2)),
+            dma((G, 2)),
+            dma((G,)),
+            dma((G,)),
             dma((G, 2, 2)),
             dma((G, 2, 2)),
-            dma((G,)),
-            dma((G,)),
-            dma((G, 3, 2)),
-            dma((G, 3, 2)),
             dma((G, 2)),
             dma((G, 2)),
             dma((5,)),
@@ -523,7 +494,7 @@
         qkv,
         residual,
         text_kv,
-        text_len.reshape(1, 1),
+        text_len,
         text_keep,
         attn_gate,
         w_out,

time: 88.3 us -> 84.9 us (0.961)
  Pallas kernels: 86.8 us -> 83.4 us
    pallas_call x1, Pallas kernels: 84.3 us -> 80.9 us  [shards(): pl.pallas_call(body, out_shape=(jax.ShapeDtypeStruct((ROWS, 64), F32), ja...]
where the time goes in v6:
time: 84.9 us; the launch traced here: 84.6 us
  Pallas kernels  83.4 us (98%)
  between operations  1.29 us (2%)
    pallas_call x1, Pallas kernels, shards(): pl.pallas_call(body, out_shape=(jax.ShapeDtypeStruct((ROWS, 64), F32), ja...  80.9 us
    pallas_call x1, Pallas kernels, shards(): pl.pallas_call(conv_body, out_shape=(jax.ShapeDtypeStruct((2, 64, 64), F3...  2.43 us

profile of v6, /device:TPU:3, one launch (start us, length us, event | category | flops | bytes accessed | tf_op | source)
XLA Modules:
  0.0 84.6 jit_solution(6223279606061148925)
XLA Ops:
  1.3 80.9 %shard_map.131 = (f32[128,64]{1,0:T(8,128)}, bf16[2,128,64]{2,1,0:T(8,128)(2,1)}) custom-call(bf16[1,2,64,9216]{3,2,1,0:T(8,128)(2,1)} %qkv.1, bf16[1,2,64,3072]{3,2,1,0:T(8,128)(2,1)} %residual.1, bf16[1,256,2,24,128]{4,3,2,1,0:T(8,128)(2,1)} %text_kv.1, s32[1]{0:T(128)S(6)} %copy.14.tlen, s32[1,256]{1,0:T(1,128)} %keep.1, f32[1,3072]{1,0:T(1,128)} %gate.1, ...), custom_call_target="tpu_custom_call" | custom-call | tf_op jit(solution)/shard_map/pallas_call | solution.py:440
  82.2 2.4 %shard_map.132 = (f32[2,64,64]{2,1,0:T(8,128)}, bf16[2,64,2,512]{3,2,1,0:T(2,128)(2,1)}) custom-call(f32[128,64]{1,0:T(8,128)} %get-tuple-element.4.guided, bf16[2,128,64]{2,1,0:T(8,128)(2,1)} %get-tuple-element.5.latents, bf16[48,512]{1,0:T(8,128)(2,1)} %bitcast.6, f32[1,512]{1,0:T(1,128)} %bitcast.7), custom_call_target="tpu_custom_call" | custom-call | tf_op jit(solution)/shard_map/pallas_call | solution.py:505

commit v7 on v6

--- a/solution.py
+++ b/solution.py
@@ -440,8 +440,8 @@
     guided, latents = pl.pallas_call(
         body,
         out_shape=(
-            jax.ShapeDtypeStruct((ROWS, 64), F32),
-            jax.ShapeDtypeStruct((2, ROWS, 64), BF),
+            pltpu.VMEM((ROWS, 64), F32),
+            pltpu.VMEM((2, ROWS, 64), BF),
         ),
         in_specs=[hbm, hbm, hbm, vmem, vmem, vmem, hbm, vmem, hbm, vmem],
         out_specs=(vmem, vmem),

time: 84.9 us -> 85.4 us (level)
  local copies, waits for them, and re-layouts: 0 us -> 1.23 us
    unnamed x0 -> x4, local copies, waits for them, and re-layouts: none -> 1.23 us
where the time goes in v7:
time: 85.4 us; the launch traced here: 85.2 us
  Pallas kernels  82.7 us (97%)
  between operations  1.3 us (2%)
  local copies, waits for them, and re-layouts  1.23 us (1%)
    pallas_call x1, Pallas kernels, shards(): pl.pallas_call(body, out_shape=(pltpu.VMEM((ROWS, 64), F32), pltpu.VMEM((...  80.3 us
    pallas_call x1, Pallas kernels, shards(): pl.pallas_call(conv_body, out_shape=(jax.ShapeDtypeStruct((2, 64, 64), F3...  2.43 us

profile of v7, /device:TPU:3, one launch (start us, length us, event | category | flops | bytes accessed | tf_op | source)
XLA Modules:
  0.0 85.2 jit_solution(959647196047995254)
XLA Ops:
  1.3 80.3 %shard_map.131 = (f32[128,64]{1,0:T(8,128)S(1)}, bf16[2,128,64]{2,1,0:T(8,128)(2,1)S(1)}) custom-call(bf16[1,2,64,9216]{3,2,1,0:T(8,128)(2,1)} %qkv.1, bf16[1,2,64,3072]{3,2,1,0:T(8,128)(2,1)} %residual.1, bf16[1,256,2,24,128]{4,3,2,1,0:T(8,128)(2,1)} %text_kv.1, s32[1]{0:T(128)S(6)} %copy.14.tlen, s32[1,256]{1,0:T(1,128)} %keep.1, f32[1,3072]{1,0:T(1,128)} %gate.1, ...), custom_call_target="tpu_custom_call" | custom-call | tf_op jit(solution)/shard_map/pallas_call | solution.py:440
  81.6 0.0 copy-start
  81.6 0.6 copy-done
  82.2 0.0 copy-start.1
  82.2 0.6 copy-done.1
  82.8 2.4 %shard_map.132 = (f32[2,64,64]{2,1,0:T(8,128)}, bf16[2,64,2,512]{3,2,1,0:T(2,128)(2,1)}) custom-call(f32[128,64]{1,0:T(8,128)} %copy-done, bf16[2,128,64]{2,1,0:T(8,128)(2,1)} %copy-done.1, bf16[48,512]{1,0:T(8,128)(2,1)} %bitcast.6, f32[1,512]{1,0:T(1,128)} %bitcast.7), custom_call_target="tpu_custom_call" | custom-call | tf_op jit(solution)/shard_map/pallas_call | solution.py:505
Async XLA Ops:
  81.6 0.6 copy-start
  82.2 0.6 copy-start.1
